TPU v7x, 32 devices: a whole 2x2x4 slice. The times are simulated.
32 devices in a mesh: seq: 8 (over z, y), ch: 4 (over x, core).
Axes of the slice: x: 2, y: 2, z: 4, core: 2. Of those that a mesh axis runs over, the one named last changes fastest.
Arguments:
- queries: bfloat16 [8192, 8192], P('seq', 'ch'), may hold values from -6 to 6
- keys: bfloat16 [8192, 8192], P('seq', 'ch'), may hold values from -6 to 6
- values: bfloat16 [8192, 8192], P('seq', 'ch'), may hold values from -6 to 6
- filters: bfloat16 [512, 128], P('ch'), may hold values from -0.5 to 0.5
- grad_out: bfloat16 [8192, 4096], P('seq', 'ch'), may hold values from -6 to 6
- out_weight: bfloat16 [4096, 8192], P('seq', 'ch'), may hold values from -0.09375 to 0.09375
Outputs:
- grad_queries: bfloat16 [8192, 8192], P('seq', 'ch')
- grad_keys: bfloat16 [8192, 8192], P('seq', 'ch')
- grad_values: bfloat16 [8192, 8192], P('seq', 'ch')
- grad_filters: float32 [512, 128], P('ch', 'seq')
- grad_weight: bfloat16 [4096, 8192], P('seq', 'ch')
All inputs are finite; a program needn't handle non-finite values.
Results may differ from a plain program's by a relative error of at most 0.022.
Values may be sent and summed in bfloat16 or wider, within the bound.
No kernel may reach another device: no remote copies, remote signals or barrier semaphores. Data moves between devices by JAX's collectives and lax.ppermute only.
A program may use at most 192 MiB of HBM per device.

v0:
```python
import functools

import jax
import jax.numpy as jnp
from jax import lax
from jax.experimental import pallas as pl
from jax.experimental.pallas import tpu as pltpu
from jax.sharding import PartitionSpec as P

GROUP = 16
FILT = 128
LANES = 128
GPT = LANES // GROUP
LINE = 4
F32 = jnp.float32
BF16 = jnp.bfloat16
VMEM_LIMIT = 48 * 1024 * 1024


def params():
    return pltpu.CompilerParams(vmem_limit_bytes=VMEM_LIMIT)


def cost(flops, nbytes):
    return pl.CostEstimate(flops=int(flops) // 64, bytes_accessed=int(nbytes) // 64, transcendentals=0)


def fence(*arrays):
    return lax.optimization_barrier(arrays)


def after(x, *others):
    return lax.optimization_barrier((x, *others))[0]


def table_kernel(back_ref, ahead_ref, back_out, ahead_out):
    for seed, out in ((back_ref, back_out), (ahead_ref, ahead_out)):
        for g in range(GPT):
            rows = jnp.broadcast_to(seed[g : g + 1, :], (FILT, 2 * FILT))
            turned = pltpu.roll(rows, 0, 1, stride=1, stride_axis=0)
            out[g * FILT : (g + 1) * FILT, :] = turned.astype(BF16)


def tables(filters):
    groups = filters.shape[0]
    taps = filters.astype(F32)
    back = jnp.concatenate(
        [jnp.zeros((groups, 1), F32), taps[:, ::-1], jnp.zeros((groups, FILT - 1), F32)], axis=1
    )
    ahead = jnp.concatenate([taps, jnp.zeros((groups, FILT), F32)], axis=1)
    seed = pl.BlockSpec((GPT, 2 * FILT), lambda i: (i, 0))
    full = pl.BlockSpec((GPT * FILT, 2 * FILT), lambda i: (i, 0))
    shape = jax.ShapeDtypeStruct((groups * FILT, 2 * FILT), BF16)
    return pl.pallas_call(
        table_kernel,
        grid=(groups // GPT,),
        in_specs=[seed, seed],
        out_specs=[full, full],
        out_shape=[shape, shape],
        compiler_params=params(),
        cost_estimate=cost(groups * 2**18, groups * 2**17),
    )(back, ahead)


def group_of_lane(rows, cols):
    return (lax.broadcasted_iota(jnp.int32, (rows, cols), 1) % LANES) // GROUP


def windows(ext, b):
    lo = b * FILT
    return jnp.concatenate([ext[lo : lo + 2 * FILT], ext[lo + FILT : lo + 3 * FILT]], axis=1)


def toeplitz(table, ext, blocks):
    group = group_of_lane(FILT, 2 * LANES)
    rows = []
    for b in range(0, blocks, 2):
        out = jnp.dot(table, windows(ext, b), preferred_element_type=F32)
        picked = out[:FILT]
        for g in range(1, GPT):
            picked = jnp.where(group == g, out[g * FILT : (g + 1) * FILT], picked)
        rows += [picked[:, :LANES], picked[:, LANES:]]
    return jnp.concatenate(rows, axis=0)


def product_of(k, v):
    return (k.astype(F32) * v.astype(F32)).astype(BF16)


def forward_kernel(q, k, v, prior, table, gated, mixed_out):
    blocks = q.shape[0] // FILT
    ext = jnp.concatenate([prior[...], product_of(k[...], v[...])], axis=0)
    mixed = toeplitz(table[...], ext, blocks)
    mixed_out[...] = mixed.astype(BF16)
    gated[...] = (q[...].astype(F32) * mixed).astype(BF16)


def forward(q, k, v, prior, table, chunk, chunks):
    rows, width = q.shape
    tiles = width // LANES // chunks
    here = pl.BlockSpec((rows, LANES), lambda i: (0, chunk * tiles + i))
    out = pl.BlockSpec((rows, LANES), lambda i: (0, i))
    shape = jax.ShapeDtypeStruct((rows, width // chunks), BF16)
    return pl.pallas_call(
        forward_kernel,
        grid=(tiles,),
        in_specs=[
            here,
            here,
            here,
            pl.BlockSpec((FILT, LANES), lambda i: (0, i)),
            pl.BlockSpec((GPT * FILT, 2 * FILT), lambda i: (chunk * tiles + i, 0)),
        ],
        out_specs=[out, out],
        out_shape=[shape, shape],
        compiler_params=params(),
        cost_estimate=cost(tiles * rows * 2 * 2**18, tiles * rows * 5 * 256 + tiles * 2**19),
    )(q, k, v, prior, table)


def middle_kernel(own, others, q, k, v, mixed, prior, *rest):
    gq_out, gm_out, edge_out, taps_out = rest[-4:]
    blocks = q.shape[0] // FILT
    total = own[...].astype(F32)
    for other in others:
        total = total + other[...].astype(F32)
    gg = total.astype(BF16).astype(F32)
    gq_out[...] = (gg * mixed[...].astype(F32)).astype(BF16)
    gm = (gg * q[...].astype(F32)).astype(BF16)
    gm_out[...] = gm
    edge_out[...] = gm[:FILT]
    ext = jnp.concatenate([prior[...], product_of(k[...], v[...])], axis=0)
    wide = jnp.concatenate([gm[b * FILT : (b + 1) * FILT] for b in range(blocks)], axis=1)
    group = group_of_lane(FILT, blocks * LANES)
    stack = jnp.concatenate(
        [jnp.where(group == g, wide, jnp.zeros_like(wide)) for g in range(GPT)], axis=0
    )
    near = jnp.concatenate([ext[b * FILT : (b + 2) * FILT] for b in range(blocks)], axis=1)
    lag = lax.dot_general(stack, near, (((1,), (1,)), ((), ())), preferred_element_type=F32)
    lag = lag.reshape(GPT, FILT, 2 * FILT)
    half = FILT // 2
    while half >= 8:
        lag = lag[:, :half] + pltpu.roll(lag[:, half:], 2 * FILT - half, 2)
        half //= 2
    while half >= 1:
        lag = lag + pltpu.roll(pltpu.roll(lag, 2 * FILT - half, 2), 8 - half, 1)
        half //= 2
    taps_out[...] = lag[:, 0, :]


def middle(own, others, q, k, v, mixed, prior, filled, span):
    rows, width = q.shape
    _, local, cols, first = span
    tiles = cols // LANES
    here = pl.BlockSpec((rows, LANES), lambda i: (0, first // LANES + i))
    part = pl.BlockSpec((rows, LANES), lambda i: (0, i))
    edge = pl.BlockSpec((FILT, LANES), lambda i: (0, i))
    n_other = len(others)

    def kernel(own_ref, *refs):
        middle_kernel(own_ref, refs[:n_other], *refs[n_other:])

    args = [own, *others, q, k, v, mixed, prior]
    in_specs = [part] * (1 + n_other) + [here] * 3
    in_specs.append(pl.BlockSpec((rows, LANES), lambda i: (0, local // LANES + i)))
    in_specs.append(pl.BlockSpec((FILT, LANES), lambda i: (0, local // LANES + i)))
    aliases = {}
    if filled is not None:
        aliases = {len(args): 0}
        args.append(filled)
        in_specs.append(pl.BlockSpec(memory_space=pl.ANY))
    return pl.pallas_call(
        kernel,
        grid=(tiles,),
        in_specs=in_specs,
        out_specs=[here, part, edge, pl.BlockSpec((GPT, 2 * FILT), lambda i: (i, 0))],
        out_shape=[
            jax.ShapeDtypeStruct((rows, width), BF16),
            jax.ShapeDtypeStruct((rows, cols), BF16),
            jax.ShapeDtypeStruct((FILT, cols), BF16),
            jax.ShapeDtypeStruct((cols // GROUP, 2 * FILT), F32),
        ],
        input_output_aliases=aliases,
        compiler_params=params(),
        cost_estimate=cost(tiles * rows * 2 * 2**18, tiles * rows * 9 * 256),
    )(*args)


def backward_kernel(gm, later, k, v, table, *rest):
    gk_out, gv_out = rest[-2:]
    blocks = gm.shape[0] // FILT
    ext = jnp.concatenate([gm[...], later[...]], axis=0)
    gp = toeplitz(table[...], ext, blocks)
    gk_out[...] = (gp * v[...].astype(F32)).astype(BF16)
    gv_out[...] = (gp * k[...].astype(F32)).astype(BF16)


def backward(gm, later, k, v, table, filled, span):
    rows, width = k.shape
    _, _, cols, first = span
    tiles = cols // LANES
    here = pl.BlockSpec((rows, LANES), lambda i: (0, first // LANES + i))
    part = pl.BlockSpec((rows, LANES), lambda i: (0, i))
    args = [gm, later, k, v, table]
    in_specs = [
        part,
        pl.BlockSpec((FILT, LANES), lambda i: (0, i)),
        here,
        here,
        pl.BlockSpec((GPT * FILT, 2 * FILT), lambda i: (first // LANES + i, 0)),
    ]
    aliases = {}
    if filled is not None:
        aliases = {len(args): 0, len(args) + 1: 1}
        args += filled
        in_specs += [pl.BlockSpec(memory_space=pl.ANY)] * 2
    shape = jax.ShapeDtypeStruct((rows, width), BF16)
    return pl.pallas_call(
        backward_kernel,
        grid=(tiles,),
        in_specs=in_specs,
        out_specs=[here, here],
        out_shape=[shape, shape],
        input_output_aliases=aliases,
        compiler_params=params(),
        cost_estimate=cost(tiles * rows * 2 * 2**18, tiles * rows * 5 * 256 + tiles * 2**19),
    )(*args)


def gate_kernel(pick, *refs):
    own, up, down, second, third, out = refs[LINE:]
    slots = (
        own[...],
        jnp.where(pick[LINE] == 1, down[...], up[...]),
        second[...],
        jnp.where(pick[LINE + 1] == 1, third[...], down[...]),
    )
    cot = jnp.concatenate([ref[0] for ref in refs[:LINE]], axis=1)
    total = jnp.dot(cot, jnp.concatenate(slots, axis=0), preferred_element_type=F32)
    out[...] = total.astype(out.dtype)


def gate_grad(pick, cot, weights, span):
    _, rows, depth = cot.shape
    _, _, width, first = span
    tile = min(256, width)
    tiles = width // tile

    def cot_spec(j):
        return pl.BlockSpec((1, rows, depth), lambda i, pick: (pick[j], 0, 0))

    return pl.pallas_call(
        gate_kernel,
        grid_spec=pltpu.PrefetchScalarGridSpec(
            num_scalar_prefetch=1,
            grid=(tiles,),
            in_specs=[cot_spec(j) for j in range(LINE)]
            + [pl.BlockSpec((depth, tile), lambda i, pick: (0, first // tile + i))] * len(weights),
            out_specs=pl.BlockSpec((rows, tile), lambda i, pick: (0, i)),
        ),
        out_shape=jax.ShapeDtypeStruct((rows, width), BF16),
        compiler_params=params(),
        cost_estimate=cost(
            2 * rows * LINE * depth * width, 2 * LINE * depth * (rows + width) + 2 * rows * width
        ),
    )(pick, *([cot] * LINE), *weights)


def rows_kernel(n, pick, *refs):
    out = refs[-1]
    cot, gated = refs[0][0], refs[n][...]
    if n > 1:
        cot = jnp.concatenate([ref[0] for ref in refs[:n]], axis=0)
        gated = jnp.concatenate([ref[...] for ref in refs[n : 2 * n]], axis=0)
    total = lax.dot_general(cot, gated, (((0,), (0,)), ((), ())), preferred_element_type=F32)
    if len(refs) > 2 * n + 1:
        total = total + refs[2 * n][0]
    out[0] = total.astype(out.dtype)


def weight_rows(pick, cots, gateds, dtype, base=None, skip=0):
    _, rows, depth = cots[0].shape
    width = gateds[0].shape[1]
    blocks = pick.shape[0]
    tile = width if blocks > 1 else min(512, width)
    n = len(cots)
    in_specs = [pl.BlockSpec((1, rows, depth), lambda j, i, pick: (pick[j], 0, 0))] * n
    in_specs += [pl.BlockSpec((rows, tile), lambda j, i, pick: (0, i))] * n
    args = [*cots, *gateds]
    if base is not None:
        in_specs.append(pl.BlockSpec((1, depth, tile), lambda j, i, pick: (j + skip, 0, i)))
        args.append(base)
    return pl.pallas_call(
        functools.partial(rows_kernel, n),
        grid_spec=pltpu.PrefetchScalarGridSpec(
            num_scalar_prefetch=1,
            grid=(blocks, width // tile),
            in_specs=in_specs,
            out_specs=pl.BlockSpec((1, depth, tile), lambda j, i, pick: (j, 0, i)),
        ),
        out_shape=jax.ShapeDtypeStruct((blocks, depth, width), dtype),
        compiler_params=params(),
        cost_estimate=cost(2 * n * rows * depth * width, 2 * n * rows * (depth + width)),
    )(pick, *args)


def shards(seq, ch, queries, keys, values, filters, grad_out, out_weight):
    inner = seq // LINE
    rows, width = queries.shape
    depth = out_weight.shape[0]
    chunks = 2 if width % (2 * LANES) == 0 else 1
    cols = width // chunks
    place = lax.axis_index("seq")
    z, y = place // inner, place % inner

    def send(x, pairs):
        return lax.ppermute(x, "seq", pairs)

    def along_line(x, pairs):
        return send(x, [(a * inner + i, b * inner + i) for a, b in pairs for i in range(inner)])

    def around_inner(x, shift):
        return send(
            x, [(a * inner + i, a * inner + (i + shift) % inner) for a in range(LINE) for i in range(inner)]
        )

    each = range(chunks)
    up_pairs, down_pairs = [(0, 1), (1, 2), (2, 3)], [(1, 0), (2, 1), (3, 2)]

    def merge(up, down):
        return jnp.where(z >= 2, up, down)

    pick = jnp.stack(
        [
            z,
            jnp.where(z == 0, 1, z - 1),
            jnp.where(z >= 2, z - 2, z + 2),
            jnp.where(z == 3, 0, jnp.where(z == 1, 2, 3)),
            jnp.where(z == 0, 1, 0),
            jnp.where((z == 0) | (z == 3), 1, 0),
        ]
    ).astype(jnp.int32)

    def swap_gated(h):
        return [around_inner(gateds[h], r) for r in range(1, inner)]

    even = z % 2 == 0
    first_pick = jnp.where(even, 3, 0).astype(jnp.int32).reshape(1)
    rest_pick = jnp.stack(
        [
            jnp.where(z == 0, 2, jnp.where(z == 1, 3, jnp.where(z == 2, 0, 1))),
            jnp.where(even, 1, 2),
            z,
        ]
    ).astype(jnp.int32)

    def rows_own(h):
        return weight_rows(jnp.concatenate([first_pick, rest_pick]), cots[:1], [gateds[h]], F32)

    def rows_first(h):
        return weight_rows(first_pick, cots[1:], got[h], BF16, base[h])[0]

    def rows_rest(h):
        return weight_rows(rest_pick, cots[1:], got[h], BF16, base[h], 1)

    def send_first(x):
        return along_line(x, [(0, 1), (3, 2)])

    def send_second(h, came):
        x = (rest[h][0].astype(F32) + came.astype(F32)).astype(BF16)
        return along_line(x, [(0, 1), (3, 2)]), along_line(x, [(1, 2), (2, 1)])

    def send_third(h, outer_in, inner_in):
        mine, other = rest[h][1].astype(F32), first[h].astype(F32)
        outer_in, inner_in = outer_in.astype(F32), inner_in.astype(F32)
        up = jnp.where(z == 2, other, mine) + jnp.where(z == 1, outer_in, inner_in)
        down = jnp.where(z == 1, other, mine) + jnp.where(z == 1, inner_in, outer_in)
        return along_line(up.astype(BF16), up_pairs), along_line(down.astype(BF16), down_pairs)

    def last_sum(h):
        below, above = sums[h]
        return (rest[h][2].astype(F32) + below.astype(F32) + above.astype(F32)).astype(BF16)

    def shares(span):
        return [gate_grad(pick, cots[r], weights, span) for r in range(1, inner)]

    def send_shares(parts):
        return [around_inner(part, inner - r) for r, part in enumerate(parts, 1)]

    gateds, mixeds, got, sums, first, rest, base = ([None] * chunks for _ in range(7))
    later_halves = list(each[1:])
    spans = [(0, 0, cols, 0)]
    for h in later_halves:
        spans += [(h, lo, cols // 2, h * cols + lo) for lo in (0, cols // 2)]
    parts, others, owns, gms, laters, taps = ([None] * len(spans) for _ in range(6))

    priors = []
    for h in each:
        tail = (slice(rows - FILT, rows), slice(h * cols, (h + 1) * cols))
        priors.append(product_of(keys[tail], values[tail]))
    cot_here = after(grad_out, *priors)
    next_pairs = [(i, i + 1) for i in range(seq - 1)]
    priors[0] = send(priors[0], next_pairs)
    paired = inner == 2 and ch == LINE
    other = cot_here
    cots = []
    if paired:
        kept = lax.dynamic_slice(cot_here, (0, y * depth), (rows, depth))
        other = lax.dynamic_slice(cot_here, (0, (1 - y) * depth), (rows, depth))
        cots = [lax.all_gather(kept, "ch", axis=0, tiled=False)]
    back, ahead = tables(filters)
    priors, other, weight = fence(priors, other, out_weight)
    for h in later_halves:
        priors[h] = send(priors[h], next_pairs)

    up1, down1 = along_line(weight, up_pairs), along_line(weight, down_pairs)
    swapped = around_inner(other, 1) if paired else other
    for h in each:
        gateds[h], mixeds[h] = forward(queries, keys, values, priors[h], back, h, chunks)
    if paired:
        base[0] = rows_own(0)
    up1, down1, swapped, gateds, cots, priors, base = fence(
        up1, down1, swapped, gateds, cots, priors, base
    )

    up2 = along_line(up1, [(1, 2), (2, 3)])
    down2 = along_line(down1, [(2, 1), (1, 0)])
    if paired:
        cots.append(lax.all_gather(swapped, "ch", axis=0, tiled=False))
    else:
        full = lax.all_gather(swapped, "ch", axis=1, tiled=True)
        full = full.reshape(rows, LINE, inner, depth).transpose(2, 1, 0, 3)
        for shift in range(inner):
            part = lax.dynamic_index_in_dim(full, (y + shift) % inner, 0, keepdims=False)
            cots.append(part if shift == 0 else around_inner(part, shift))
        base[0] = rows_own(0)
    for h in each:
        got[h] = swap_gated(h)

    got[0], cots, gateds, base = fence(got[0], cots, gateds, base)
    first[0] = rows_first(0)
    sums[0] = send_first(first[0])
    up2, down2, first[0] = fence(up2, down2, first[0])

    second = merge(up2, down2)
    third = along_line(second, [(2, 3), (1, 0)])
    rest[0] = rows_rest(0)
    sums[0], rest[0], gateds = fence(sums[0], rest[0], gateds)
    sums[0] = send_second(0, sums[0])
    for h in later_halves:
        base[h] = rows_own(h)
    got[1:], base = fence(got[1:], base)

    for h in later_halves:
        first[h] = rows_first(h)
        sums[h] = send_first(first[h])
    third, first = fence(third, first)
    weights = [weight, up1, down1, second, third]
    parts[0] = shares(spans[0])
    others[0] = send_shares(parts[0])

    sums[0], parts[0], third, base = fence(sums[0], parts[0], third, base)
    sums[0] = send_third(0, *sums[0])
    for h in later_halves:
        rest[h] = rows_rest(h)
    weights = [weight, up1, down1, second, third]
    for n, span in enumerate(spans[1:], 1):
        parts[n] = shares(span)
    for n in range(1, len(spans), 2):
        others[n] = send_shares(parts[n])
    sums[1:], parts, rest = fence(sums[1:], parts, rest)
    for h in later_halves:
        sums[h] = send_second(h, sums[h])
    third, _ = fence(third, parts)
    weights = [weight, up1, down1, second, third]
    owns = [gate_grad(pick, cots[0], weights, span) for span in spans]
    others[0], owns, sums[0] = fence(others[0], owns, sums[0])

    grad_queries = None
    grad_kv = None
    back_pairs = [(i + 1, i) for i in range(seq - 1)]
    done = []
    for n, span in enumerate(spans):
        half = span[0]
        grad_queries, gms[n], edge, taps[n] = middle(
            owns[n], others[n], queries, keys, values, mixeds[half], priors[half], grad_queries, span
        )
        laters[n] = send(edge, back_pairs)
        if n == 0:
            for m in range(2, len(spans), 2):
                others[m] = send_shares(after(parts[m], laters[0]))
            for g in later_halves:
                sums[g] = send_third(g, *after(sums[g], laters[0]))
            done.append(last_sum(0))
            others[1:2], owns, done = fence(others[1:2], owns, done)
        if n == 1:
            gms[0], _ = fence(gms[0], edge)
            grad_kv = backward(gms[0], laters[0], keys, values, ahead, grad_kv, spans[0])
            others[2:], grad_kv = fence(others[2:], grad_kv)
    for h in later_halves:
        sums[h], gms[1], _ = fence(sums[h], gms[1], edge)
        done.append(last_sum(h))
    for n in range(1 if len(spans) > 1 else 0, len(spans)):
        grad_kv = backward(gms[n], laters[n], keys, values, ahead, grad_kv, spans[n])
    grad_weight = jnp.concatenate(done, axis=1)
    taps = jnp.concatenate(taps, axis=0)[:, 1 : FILT + 1][:, ::-1]
    taps = taps.T.reshape(seq, FILT // seq, -1)
    taps = jnp.sum(lax.all_to_all(taps, "seq", 0, 0), axis=0)
    return grad_queries, *grad_kv, taps.T, grad_weight


def solution(mesh):
    sizes = dict(mesh.shape)
    return jax.shard_map(
        functools.partial(shards, sizes["seq"], sizes["ch"]),
        mesh=mesh,
        in_specs=(
            P("seq", "ch"),
            P("seq", "ch"),
            P("seq", "ch"),
            P("ch", None),
            P("seq", "ch"),
            P("seq", "ch"),
        ),
        out_specs=(P("seq", "ch"), P("seq", "ch"), P("seq", "ch"), P("ch", "seq"), P("seq", "ch")),
        check_vma=False,
    )
```

profile of v0, /device:TPU:10, one launch (start us, length us, event | category | flops | bytes accessed | tf_op | source)
XLA Modules:
  0.0 385.2 jit_solution(14110313094077366027)
XLA Ops:
  7.2 1.4 multiply_convert_fusion
  8.7 3.2 constant_dynamic-slice_fusion
  11.9 3.4 collective-permute-start
  15.3 7.4 %collective-permute-done.prior.refs_5_ = bf16[128,1024]{1,0:T(8,128)(2,1)S(1)} collective-permute-done((bf16[128,1024]{1,0:T(8,128)(2,1)S(1)}, bf16[128,1024]{1,0:T(8,128)(2,1)S(1)}, u32[]{:S(2)}, u32[]{:S(2)}) %collective-permute-start) | collective-permute-done | bytes 262176 | tf_op jit(solution)/shard_map/ppermute | solution.py:317
  22.8 3.5 collective-permute-start.1
  26.2 3.7 collective-permute-start.2
  30.8 3.3 collective-permute-start.4
  34.2 10.5 %shard_map.101 = (bf16[16384,256]{1,0:T(8,128)(2,1)}, bf16[16384,256]{1,0:T(8,128)(2,1)}) custom-call(f32[128,256]{1,0:T(8,128)S(1)} %maximum_maximum_fusion.back_ref, f32[128,256]{1,0:T(8,128)S(1)} %concatenate.19.ahead_ref), custom_call_target="tpu_custom_call" | custom-call | flops 524288 | bytes 262144 | tf_op jit(solution)/shard_map/pallas_call | solution.py:54
  44.7 9.9 %shard_map.102 = (bf16[1024,1024]{1,0:T(8,128)(2,1)S(1)}, bf16[1024,1024]{1,0:T(8,128)(2,1)S(1)}) custom-call(bf16[1024,2048]{1,0:T(8,128)(2,1)} %refs_1_.5, bf16[1024,2048]{1,0:T(8,128)(2,1)} %k.9, bf16[1024,2048]{1,0:T(8,128)(2,1)} %v.9, bf16[128,1024]{1,0:T(8,128)(2,1)S(1)} %collective-permute-done.prior.refs_5_, bf16[16384,256]{1,0:T(8,128)(2,1)} %get-tuple-element.92.table), custom_call_target="tpu_custom_call" | custom-call | flops 67108864 | bytes 229376 | tf_op jit(solution)/shard_map/pallas_call | solution.py:104
  54.6 1.3 copy-done.12
  55.9 1.3 copy-done.15
  57.3 19.6 %collective-permute-done.4.prior.refs_5_ = bf16[128,1024]{1,0:T(8,128)(2,1)S(1)} collective-permute-done((bf16[128,1024]{1,0:T(8,128)(2,1)S(1)}, bf16[128,1024]{1,0:T(8,128)(2,1)S(1)}, u32[]{:S(2)}, u32[]{:S(2)}) %collective-permute-start.4) | collective-permute-done | bytes 262176 | tf_op jit(solution)/shard_map/ppermute | solution.py:317
  76.8 9.9 %shard_map.103 = (bf16[1024,1024]{1,0:T(8,128)(2,1)S(1)}, bf16[1024,1024]{1,0:T(8,128)(2,1)S(1)}) custom-call(bf16[1024,2048]{1,0:T(8,128)(2,1)} %refs_1_.5, bf16[1024,2048]{1,0:T(8,128)(2,1)} %k.9, bf16[1024,2048]{1,0:T(8,128)(2,1)} %v.9, bf16[128,1024]{1,0:T(8,128)(2,1)S(1)} %collective-permute-done.4.prior.refs_5_, bf16[16384,256]{1,0:T(8,128)(2,1)} %get-tuple-element.92.table), custom_call_target="tpu_custom_call" | custom-call | flops 67108864 | bytes 229376 | tf_op jit(solution)/shard_map/pallas_call | solution.py:104
  86.7 1.3 copy-done.6
  88.0 1.3 copy-done.13
  89.4 1.6 copy-done.16
  90.9 9.0 %shard_map.104.refs_2_ = f32[4,512,1024]{2,1,0:T(8,128)} custom-call(s32[4]{0:T(128)S(1)} %pad_add_fusion.pick, bf16[4,1024,512]{2,1,0:T(8,128)(2,1)} %bitcast.57, bf16[1024,1024]{1,0:T(8,128)(2,1)S(1)} %copy-done.16), custom_call_target="tpu_custom_call" | custom-call | flops 16777216 | bytes 49152 | tf_op jit(solution)/shard_map/pallas_call | solution.py:293
  100.1 4.8 %collective-permute-start.6 = (bf16[512,2048]{1,0:T(8,128)(2,1)}, bf16[512,2048]{1,0:T(8,128)(2,1)}, u32[]{:S(2)}, u32[]{:S(2)}) collective-permute-start(bf16[512,2048]{1,0:T(8,128)(2,1)} %collective-permute-done.1.refs_5_), channel_id=1, source_target_pairs={{8,16},{12,20},{16,24},{20,28},{9,17},{13,21},{17,25},{21,29},{10,... | collective-permute-start | bytes 6291464 | tf_op jit(solution)/shard_map/ppermute | solution.py:317
  104.8 1.9 collective-permute-start.7
  106.8 2.1 collective-permute-start.12
  108.8 40.1 %collective-permute-done.5.refs_1_ = bf16[1024,1024]{1,0:T(8,128)(2,1)} collective-permute-done((bf16[1024,1024]{1,0:T(8,128)(2,1)}, bf16[1024,1024]{1,0:T(8,128)(2,1)}, u32[]{:S(2)}, u32[]{:S(2)}) %collective-permute-start.5) | collective-permute-done | bytes 2097184 | tf_op jit(solution)/shard_map/ppermute | solution.py:317
  148.9 3.4 shard_map.105
  152.4 3.5 broadcast_select_fusion.refs_7_
  155.9 3.0 collective-permute-start.11
  160.3 7.6 %shard_map.106 = bf16[3,512,1024]{2,1,0:T(8,128)(2,1)S(1)} custom-call(s32[3]{0:T(128)S(1)} %pad_add_fusion.1.pick, bf16[4,1024,512]{2,1,0:T(8,128)(2,1)} %bitcast.42, bf16[1024,1024]{1,0:T(8,128)(2,1)} %collective-permute-done.5.refs_1_, f32[4,512,1024]{2,1,0:T(8,128)} %shard_map.104.refs_2_), custom_call_target="tpu_custom_call" | custom-call | flops 16777216 | bytes 49152 | tf_op jit(solution)/shard_map/pallas_call | solution.py:293
  168.0 14.7 %collective-permute-done.8 = bf16[512,1024]{1,0:T(8,128)(2,1)S(1)} collective-permute-done((bf16[512,1024]{1,0:T(8,128)(2,1)S(1)}, bf16[512,1024]{1,0:T(8,128)(2,1)S(1)}, u32[]{:S(2)}, u32[]{:S(2)}) %collective-permute-start.8) | collective-permute-done | bytes 1048608 | tf_op jit(solution)/shard_map/ppermute | solution.py:317
  182.7 1.4 fusion.13
  184.1 2.2 collective-permute-start.10
  187.7 9.0 %shard_map.107.refs_2_ = f32[4,512,1024]{2,1,0:T(8,128)} custom-call(s32[4]{0:T(128)S(1)} %pad_add_fusion.pick, bf16[4,1024,512]{2,1,0:T(8,128)(2,1)} %bitcast.58, bf16[1024,1024]{1,0:T(8,128)(2,1)S(1)} %copy-done.14), custom_call_target="tpu_custom_call" | custom-call | flops 16777216 | bytes 49152 | tf_op jit(solution)/shard_map/pallas_call | solution.py:293
  196.7 3.4 shard_map.108
  200.1 1.5 collective-permute-start.15
  201.7 8.6 %shard_map.109 = bf16[1024,1024]{1,0:T(8,128)(2,1)S(1)} custom-call(s32[6]{0:T(128)S(1)} %stack.37.pick, bf16[4,1024,512]{2,1,0:T(8,128)(2,1)} %bitcast.44, bf16[4,1024,512]{2,1,0:T(8,128)(2,1)} %bitcast.45, bf16[4,1024,512]{2,1,0:T(8,128)(2,1)} %bitcast.46, bf16[4,1024,512]{2,1,0:T(8,128)(2,1)} %bitcast.47, bf16[512,2048]{1,0:T(8,128)(2,1)S(1)} %copy-done.2, ...), custom_call_target="tpu_custom_call" | custom-call | flops 67108864 | bytes 163840 | tf_op jit(solution)/shard_map/pallas_call | solution.py:252
  211.5 3.1 collective-permute-done.9
  214.7 7.6 %shard_map.112 = bf16[3,512,1024]{2,1,0:T(8,128)(2,1)S(1)} custom-call(s32[3]{0:T(128)S(1)} %pad_add_fusion.1.pick, bf16[4,1024,512]{2,1,0:T(8,128)(2,1)} %bitcast.48, bf16[1024,1024]{1,0:T(8,128)(2,1)} %collective-permute-done.12.refs_1_, f32[4,512,1024]{2,1,0:T(8,128)} %shard_map.107.refs_2_), custom_call_target="tpu_custom_call" | custom-call | flops 16777216 | bytes 49152 | tf_op jit(solution)/shard_map/pallas_call | solution.py:293
  222.3 6.2 %shard_map.111 = bf16[1024,512]{1,0:T(8,128)(2,1)S(1)} custom-call(s32[6]{0:T(128)S(1)} %stack.37.pick, bf16[4,1024,512]{2,1,0:T(8,128)(2,1)} %bitcast.49, bf16[4,1024,512]{2,1,0:T(8,128)(2,1)} %bitcast.50, bf16[4,1024,512]{2,1,0:T(8,128)(2,1)} %bitcast.51, bf16[4,1024,512]{2,1,0:T(8,128)(2,1)} %bitcast.52, bf16[512,2048]{1,0:T(8,128)(2,1)S(1)} %copy-done.2, ...), custom_call_target="tpu_custom_call" | custom-call | flops 33554432 | bytes 114688 | tf_op jit(solution)/shard_map/pallas_call | solution.py:252
  229.5 6.0 %shard_map.110 = bf16[1024,512]{1,0:T(8,128)(2,1)S(1)} custom-call(s32[6]{0:T(128)S(1)} %stack.37.pick, bf16[4,1024,512]{2,1,0:T(8,128)(2,1)} %bitcast.53, bf16[4,1024,512]{2,1,0:T(8,128)(2,1)} %bitcast.54, bf16[4,1024,512]{2,1,0:T(8,128)(2,1)} %bitcast.55, bf16[4,1024,512]{2,1,0:T(8,128)(2,1)} %bitcast.56, bf16[512,2048]{1,0:T(8,128)(2,1)S(1)} %copy-done.2, ...), custom_call_target="tpu_custom_call" | custom-call | flops 33554432 | bytes 114688 | tf_op jit(solution)/shard_map/pallas_call | solution.py:252
  235.6 4.3 %fusion.3 = (bf16[512,1024]{1,0:T(8,128)(2,1)}, bf16[512,1024]{1,0:T(8,128)(2,1)}) fusion(bf16[512,1024]{1,0:T(8,128)(2,1)} %collective-permute-done.9, bf16[512,1024]{1,0:T(8,128)(2,1)} %collective-permute-done.10, bf16[512,1024]{1,0:T(8,128)(2,1)S(1)} %bitcast.40, pred[]{:T(512)S(6)} %eq.15, bf16[3,512,1024]{2,1,0:T(8,128)(2,1)S(1)} %copy-done.4, pred[]{:T(512)S(6)} %eq.17), kind=kLoop, calls=%fused_computation.11 | loop fusion | flops 6291456 | bytes 6291458 | tf_op jit(solution)/shard_map/convert_element_type | solution.py:378
  240.0 3.6 collective-permute-start.16
  243.6 3.2 collective-permute-start.17
  246.8 2.6 fusion.10
  250.7 2.7 collective-permute-start.22
  253.4 5.8 %shard_map.115.own_ref = bf16[1024,512]{1,0:T(8,128)(2,1)S(1)} custom-call(s32[6]{0:T(128)S(1)} %stack.37.pick, bf16[4,1024,512]{2,1,0:T(8,128)(2,1)} %bitcast.59, bf16[4,1024,512]{2,1,0:T(8,128)(2,1)} %bitcast.60, bf16[4,1024,512]{2,1,0:T(8,128)(2,1)} %bitcast.61, bf16[4,1024,512]{2,1,0:T(8,128)(2,1)} %bitcast.62, bf16[512,2048]{1,0:T(8,128)(2,1)S(1)} %copy-done.2, ...), custom_call_target="tpu_custom_call" | custom-call | flops 33554432 | bytes 114688 | tf_op jit(solution)/shard_map/pallas_call | solution.py:252
  259.2 5.8 %shard_map.114.own_ref = bf16[1024,512]{1,0:T(8,128)(2,1)S(1)} custom-call(s32[6]{0:T(128)S(1)} %stack.37.pick, bf16[4,1024,512]{2,1,0:T(8,128)(2,1)} %bitcast.63, bf16[4,1024,512]{2,1,0:T(8,128)(2,1)} %bitcast.64, bf16[4,1024,512]{2,1,0:T(8,128)(2,1)} %bitcast.65, bf16[4,1024,512]{2,1,0:T(8,128)(2,1)} %bitcast.66, bf16[512,2048]{1,0:T(8,128)(2,1)S(1)} %copy-done.2, ...), custom_call_target="tpu_custom_call" | custom-call | flops 33554432 | bytes 114688 | tf_op jit(solution)/shard_map/pallas_call | solution.py:252
  265.9 8.6 %shard_map.113.own_ref = bf16[1024,1024]{1,0:T(8,128)(2,1)S(1)} custom-call(s32[6]{0:T(128)S(1)} %stack.37.pick, bf16[4,1024,512]{2,1,0:T(8,128)(2,1)} %bitcast.67, bf16[4,1024,512]{2,1,0:T(8,128)(2,1)} %bitcast.68, bf16[4,1024,512]{2,1,0:T(8,128)(2,1)} %bitcast.69, bf16[4,1024,512]{2,1,0:T(8,128)(2,1)} %bitcast.70, bf16[512,2048]{1,0:T(8,128)(2,1)S(1)} %copy-done.2, ...), custom_call_target="tpu_custom_call" | custom-call | flops 67108864 | bytes 163840 | tf_op jit(solution)/shard_map/pallas_call | solution.py:252
  274.5 12.7 %shard_map.116 = (bf16[1024,2048]{1,0:T(8,128)(2,1)}, bf16[1024,1024]{1,0:T(8,128)(2,1)S(1)}, bf16[128,1024]{1,0:T(8,128)(2,1)S(1)}, f32[64,256]{1,0:T(8,128)S(1)}) custom-call(bf16[1024,1024]{1,0:T(8,128)(2,1)S(1)} %shard_map.113.own_ref, bf16[1024,1024]{1,0:T(8,128)(2,1)} %collective-permute-done.14.refs_0_, bf16[1024,2048]{1,0:T(8,128)(2,1)} %refs_1_.5, ...), custom_call_target="tpu_custom_call" | custom-call | flops 67108864 | bytes 294912 | tf_op jit(solution)/shard_map/pallas_call | solution.py:172
  287.2 5.0 %collective-permute-start.18 = (bf16[128,1024]{1,0:T(8,128)(2,1)S(1)}, bf16[128,1024]{1,0:T(8,128)(2,1)S(1)}, u32[]{:S(2)}, u32[]{:S(2)}) collective-permute-start(bf16[128,1024]{1,0:T(8,128)(2,1)S(1)} %get-tuple-element.134), channel_id=1, source_target_pairs={{4,0},{8,4},{12,8},{16,12},{20,16},{24,20},{28,24},{5,1},{9,5},{13... | collective-permute-start | bytes 786440 | tf_op jit(solution)/shard_map/ppermute | solution.py:317
  292.4 6.0 %collective-permute-done.18.later = bf16[128,1024]{1,0:T(8,128)(2,1)S(1)} collective-permute-done((bf16[128,1024]{1,0:T(8,128)(2,1)S(1)}, bf16[128,1024]{1,0:T(8,128)(2,1)S(1)}, u32[]{:S(2)}, u32[]{:S(2)}) %collective-permute-start.18) | collective-permute-done | bytes 262176 | tf_op jit(solution)/shard_map/ppermute | solution.py:317
  298.4 4.0 %fusion.7 = (bf16[512,1024]{1,0:T(8,128)(2,1)}, bf16[512,1024]{1,0:T(8,128)(2,1)}) fusion(bf16[512,1024]{1,0:T(8,128)(2,1)} %collective-permute-done.21, bf16[512,1024]{1,0:T(8,128)(2,1)} %collective-permute-done.22, bf16[512,1024]{1,0:T(8,128)(2,1)S(1)} %bitcast.38, pred[]{:T(512)S(6)} %eq.15, bf16[3,512,1024]{2,1,0:T(8,128)(2,1)S(1)} %shard_map.112, ...), kind=kLoop, calls=%fused_computation.15 | loop fusion | flops 6291456 | bytes 6291458 | tf_op jit(solution)/shard_map/convert_element_type | solution.py:378
  302.4 3.1 collective-permute-start.23
  305.5 4.1 %collective-permute-start.24 = (bf16[512,1024]{1,0:T(8,128)(2,1)}, bf16[512,1024]{1,0:T(8,128)(2,1)}, u32[]{:S(2)}, u32[]{:S(2)}) collective-permute-start(bf16[512,1024]{1,0:T(8,128)(2,1)} %get-tuple-element.173), channel_id=1, source_target_pairs={{8,0},{12,4},{16,8},{20,12},{24,16},{28,20},{9,1},{13,5},{17,9},{2... | collective-permute-start | bytes 3145736 | tf_op jit(solution)/shard_map/ppermute | solution.py:317
  309.7 3.2 fusion.12
  312.9 8.0 %collective-permute-done.13.refs_0_ = bf16[1024,512]{1,0:T(8,128)(2,1)S(1)} collective-permute-done((bf16[1024,512]{1,0:T(8,128)(2,1)S(1)}, bf16[1024,512]{1,0:T(8,128)(2,1)S(1)}, u32[]{:S(2)}, u32[]{:S(2)}) %collective-permute-start.13) | collective-permute-done | bytes 1048608 | tf_op jit(solution)/shard_map/ppermute | solution.py:317
  320.8 7.5 %shard_map.117 = (bf16[1024,2048]{1,0:T(8,128)(2,1)}, bf16[1024,512]{1,0:T(8,128)(2,1)S(1)}, bf16[128,512]{1,0:T(8,128)(2,1)}, f32[32,256]{1,0:T(8,128)S(1)}) custom-call(bf16[1024,512]{1,0:T(8,128)(2,1)S(1)} %copy-done.11, bf16[1024,512]{1,0:T(8,128)(2,1)S(1)} %collective-permute-done.13.refs_0_, ...), custom_call_target="tpu_custom_call", output_to_operand_aliasing={{0}: (7, {})} | custom-call | flops 33554432 | bytes 147456 | tf_op jit(solution)/shard_map/pallas_call | solution.py:172
  328.3 3.4 collective-permute-start.25
  331.7 10.5 %shard_map.118 = (bf16[1024,2048]{1,0:T(8,128)(2,1)}, bf16[1024,2048]{1,0:T(8,128)(2,1)}) custom-call(bf16[1024,1024]{1,0:T(8,128)(2,1)S(1)} %get-tuple-element.143.gm, bf16[128,1024]{1,0:T(8,128)(2,1)S(1)} %collective-permute-done.18.later, bf16[1024,2048]{1,0:T(8,128)(2,1)} %k.9, bf16[1024,2048]{1,0:T(8,128)(2,1)} %v.9, ...), custom_call_target="tpu_custom_call" | custom-call | flops 67108864 | bytes 229376 | tf_op jit(solution)/shard_map/pallas_call | solution.py:218
  342.2 7.5 %shard_map.119 = (bf16[1024,2048]{1,0:T(8,128)(2,1)}, bf16[1024,512]{1,0:T(8,128)(2,1)S(1)}, bf16[128,512]{1,0:T(8,128)(2,1)}, f32[32,256]{1,0:T(8,128)S(1)}) custom-call(bf16[1024,512]{1,0:T(8,128)(2,1)S(1)} %shard_map.115.own_ref, bf16[1024,512]{1,0:T(8,128)(2,1)S(1)} %collective-permute-done.19.refs_0_, ...), custom_call_target="tpu_custom_call", output_to_operand_aliasing={{0}: (7, {})} | custom-call | flops 33554432 | bytes 147456 | tf_op jit(solution)/shard_map/pallas_call | solution.py:172
  349.7 4.4 %collective-permute-start.20 = (bf16[128,512]{1,0:T(8,128)(2,1)}, bf16[128,512]{1,0:T(8,128)(2,1)S(1)}, u32[]{:S(2)}, u32[]{:S(2)}) collective-permute-start(bf16[128,512]{1,0:T(8,128)(2,1)} %get-tuple-element.151), channel_id=1, source_target_pairs={{4,0},{8,4},{12,8},{16,12},{20,16},{24,20},{28,24},{5,1},{9,5},{13... | collective-permute-start | bytes 393224 | tf_op jit(solution)/shard_map/ppermute | solution.py:317
  355.0 3.3 all-to-all-start
  358.3 2.6 fusion.9
  360.9 1.5 pad_maximum_fusion
  362.4 1.4 copy-done
  363.8 5.8 %shard_map.120 = (bf16[1024,2048]{1,0:T(8,128)(2,1)}, bf16[1024,2048]{1,0:T(8,128)(2,1)}) custom-call(bf16[1024,512]{1,0:T(8,128)(2,1)S(1)} %get-tuple-element.158.gm, bf16[128,512]{1,0:T(8,128)(2,1)S(1)} %collective-permute-done.25.later, bf16[1024,2048]{1,0:T(8,128)(2,1)S(1)} %copy-done, ...), custom_call_target="tpu_custom_call", output_to_operand_aliasing={{0}: (5, {}), {1}: (6, {})} | custom-call | flops 33554432 | bytes 114688 | tf_op jit(solution)/shard_map/pallas_call | solution.py:218
  370.3 2.2 copy-done.1
  372.5 5.8 %shard_map.121 = (bf16[1024,2048]{1,0:T(8,128)(2,1)}, bf16[1024,2048]{1,0:T(8,128)(2,1)}) custom-call(bf16[1024,512]{1,0:T(8,128)(2,1)S(1)} %copy-done.18, bf16[128,512]{1,0:T(8,128)(2,1)S(1)} %collective-permute-done.20.later, bf16[1024,2048]{1,0:T(8,128)(2,1)S(1)} %copy-done.1, ...), custom_call_target="tpu_custom_call", output_to_operand_aliasing={{0}: (5, {}), {1}: (6, {})} | custom-call | flops 33554432 | bytes 114688 | tf_op jit(solution)/shard_map/pallas_call | solution.py:218
  (94 shorter events, 10.1 us)
Async XLA Ops:
  7.2 82.2 %all-gather.5.cloned.1.call-start = ((), (), s32[]{:S(2)}) async-start(), calls=%async_computation.1 | async-start | bytes 5242880 | tf_op jit(solution)/shard_map/all_gather | solution.py:410
  8.6 14.1 %copy-start.2 = (bf16[512,2048]{1,0:T(8,128)(2,1)S(1)}, bf16[512,2048]{1,0:T(8,128)(2,1)}, u32[]{:S(2)}) copy-start(bf16[512,2048]{1,0:T(8,128)(2,1)} %refs_4_.5) | copy-start | bytes 6291460
  8.6 21.9 %copy-start.26 = (bf16[128,128]{1,0:T(8,128)(2,1)S(1)}, bf16[128,128]{1,0:T(8,128)(2,1)}, u32[]{:S(2)}) copy-start(bf16[128,128]{1,0:T(8,128)(2,1)} %param.9) | copy-start | bytes 98308
  11.9 137.1 %all-gather.7.cloned.1.call-start = ((), (), s32[]{:S(2)}) async-start(), calls=%async_computation.2 | async-start | bytes 5242880 | tf_op jit(solution)/shard_map/all_gather | solution.py:429
  11.9 10.8 %collective-permute-start = (bf16[128,1024]{1,0:T(8,128)(2,1)S(1)}, bf16[128,1024]{1,0:T(8,128)(2,1)S(1)}, u32[]{:S(2)}, u32[]{:S(2)}) collective-permute-start(bf16[128,1024]{1,0:T(8,128)(2,1)S(1)} %get-tuple-element.172), channel_id=1, source_target_pairs={{0,4},{4,8},{8,12},{12,16},{16,20},{20,24},{24,28},{1,5},{5,9},{9,... | collective-permute-start | bytes 786440 | tf_op jit(solution)/shard_map/ppermute | solution.py:317
  22.7 31.9 %copy-start.19 = (bf16[128,1024]{1,0:T(8,128)(2,1)}, bf16[128,1024]{1,0:T(8,128)(2,1)S(1)}, u32[]{:S(2)}) copy-start(bf16[128,1024]{1,0:T(8,128)(2,1)S(1)} %collective-permute-done.prior.refs_5_) | copy-start | bytes 786436
  22.8 77.2 %collective-permute-start.1 = (bf16[512,2048]{1,0:T(8,128)(2,1)S(1)}, bf16[512,2048]{1,0:T(8,128)(2,1)}, u32[]{:S(2)}, u32[]{:S(2)}) collective-permute-start(bf16[512,2048]{1,0:T(8,128)(2,1)S(1)} %copy-done.2), channel_id=1, source_target_pairs={{0,8},{4,12},{8,16},{12,20},{16,24},{20,28},{1,9},{5,13},{9,17},{1... | collective-permute-start | bytes 6291464 | tf_op jit(solution)/shard_map/ppermute | solution.py:317
  26.2 73.7 %collective-permute-start.2 = (bf16[512,2048]{1,0:T(8,128)(2,1)S(1)}, bf16[512,2048]{1,0:T(8,128)(2,1)}, u32[]{:S(2)}, u32[]{:S(2)}) collective-permute-start(bf16[512,2048]{1,0:T(8,128)(2,1)S(1)} %copy-done.2), channel_id=1, source_target_pairs={{8,0},{12,4},{16,8},{20,12},{24,16},{28,20},{9,1},{13,5},{17,9},{2... | collective-permute-start | bytes 6291464 | tf_op jit(solution)/shard_map/ppermute | solution.py:317
  29.9 70.0 %collective-permute-start.3 = (bf16[1024,512]{1,0:T(8,128)(2,1)}, bf16[1024,512]{1,0:T(8,128)(2,1)}, u32[]{:S(2)}, u32[]{:S(2)}) collective-permute-start(bf16[1024,512]{1,0:T(8,128)(2,1)} %get-tuple-element.90), channel_id=1, source_target_pairs={{0,4},{4,0},{8,12},{12,8},{16,20},{20,16},{24,28},{28,24},{1,5},{5... | collective-permute-start | bytes 3145736 | tf_op jit(solution)/shard_map/ppermute | solution.py:317
  30.8 46.0 %collective-permute-start.4 = (bf16[128,1024]{1,0:T(8,128)(2,1)S(1)}, bf16[128,1024]{1,0:T(8,128)(2,1)S(1)}, u32[]{:S(2)}, u32[]{:S(2)}) collective-permute-start(bf16[128,1024]{1,0:T(8,128)(2,1)S(1)} %get-tuple-element.94), channel_id=1, source_target_pairs={{0,4},{4,8},{8,12},{12,16},{16,20},{20,24},{24,28},{1,5},{5,9},{9,... | collective-permute-start | bytes 786440 | tf_op jit(solution)/shard_map/ppermute | solution.py:317
  54.6 1.3 copy-start.12
  55.9 1.3 copy-start.15
  86.7 1.3 copy-start.6
  88.0 1.3 copy-start.13
  89.4 1.6 copy-start.16
  100.0 48.9 %collective-permute-start.5 = (bf16[1024,1024]{1,0:T(8,128)(2,1)}, bf16[1024,1024]{1,0:T(8,128)(2,1)}, u32[]{:S(2)}, u32[]{:S(2)}) collective-permute-start(bf16[1024,1024]{1,0:T(8,128)(2,1)} %copy-done.15), channel_id=1, source_target_pairs={{0,4},{4,0},{8,12},{12,8},{16,20},{20,16},{24,28},{28,24},{1,5},{5... | collective-permute-start | bytes 6291464 | tf_op jit(solution)/shard_map/ppermute | solution.py:317
  100.1 52.3 %collective-permute-start.6 = (bf16[512,2048]{1,0:T(8,128)(2,1)}, bf16[512,2048]{1,0:T(8,128)(2,1)}, u32[]{:S(2)}, u32[]{:S(2)}) collective-permute-start(bf16[512,2048]{1,0:T(8,128)(2,1)} %collective-permute-done.1.refs_5_), channel_id=1, source_target_pairs={{8,16},{12,20},{16,24},{20,28},{9,17},{13,21},{17,25},{21,29},{10,... | collective-permute-start | bytes 6291464 | tf_op jit(solution)/shard_map/ppermute | solution.py:317
  104.8 47.6 %collective-permute-start.7 = (bf16[512,2048]{1,0:T(8,128)(2,1)}, bf16[512,2048]{1,0:T(8,128)(2,1)}, u32[]{:S(2)}, u32[]{:S(2)}) collective-permute-start(bf16[512,2048]{1,0:T(8,128)(2,1)} %collective-permute-done.2.refs_6_), channel_id=1, source_target_pairs={{16,8},{20,12},{8,0},{12,4},{17,9},{21,13},{9,1},{13,5},{18,10},{2... | collective-permute-start | bytes 6291464 | tf_op jit(solution)/shard_map/ppermute | solution.py:317
  106.8 89.9 %collective-permute-start.12 = (bf16[1024,1024]{1,0:T(8,128)(2,1)}, bf16[1024,1024]{1,0:T(8,128)(2,1)}, u32[]{:S(2)}, u32[]{:S(2)}) collective-permute-start(bf16[1024,1024]{1,0:T(8,128)(2,1)} %copy-done.13), channel_id=1, source_target_pairs={{0,4},{4,0},{8,12},{12,8},{16,20},{20,16},{24,28},{28,24},{1,5},{5... | collective-permute-start | bytes 6291464 | tf_op jit(solution)/shard_map/ppermute | solution.py:317
  152.4 6.6 %copy-start.8 = (bf16[1,512,1024]{2,1,0:T(8,128)(2,1)}, bf16[1,512,1024]{2,1,0:T(8,128)(2,1)S(1)}, u32[]{:S(2)}) copy-start(bf16[1,512,1024]{2,1,0:T(8,128)(2,1)S(1)} %shard_map.105) | copy-start | bytes 3145732
  155.9 45.8 %collective-permute-start.11 = (bf16[512,2048]{1,0:T(8,128)(2,1)}, bf16[512,2048]{1,0:T(8,128)(2,1)}, u32[]{:S(2)}, u32[]{:S(2)}) collective-permute-start(bf16[512,2048]{1,0:T(8,128)(2,1)} %broadcast_select_fusion.refs_7_), channel_id=1, source_target_pairs={{16,24},{20,28},{8,0},{12,4},{17,25},{21,29},{9,1},{13,5},{18,26},... | collective-permute-start | bytes 6291464 | tf_op jit(solution)/shard_map/ppermute | solution.py:317
  159.0 23.8 %collective-permute-start.8 = (bf16[512,1024]{1,0:T(8,128)(2,1)S(1)}, bf16[512,1024]{1,0:T(8,128)(2,1)S(1)}, u32[]{:S(2)}, u32[]{:S(2)}) collective-permute-start(bf16[512,1024]{1,0:T(8,128)(2,1)S(1)} %bitcast.39), channel_id=1, source_target_pairs={{0,8},{4,12},{24,16},{28,20},{1,9},{5,13},{25,17},{29,21},{2,10},{... | collective-permute-start | bytes 3145736 | tf_op jit(solution)/shard_map/ppermute | solution.py:317
  168.0 14.8 %copy-start.3 = (bf16[3,512,1024]{2,1,0:T(8,128)(2,1)}, bf16[3,512,1024]{2,1,0:T(8,128)(2,1)S(1)}, u32[]{:S(2)}) copy-start(bf16[3,512,1024]{2,1,0:T(8,128)(2,1)S(1)} %shard_map.106) | copy-start | bytes 9437188
  168.0 19.7 %copy-start.14 = (bf16[1024,1024]{1,0:T(8,128)(2,1)S(1)}, bf16[1024,1024]{1,0:T(8,128)(2,1)}, u32[]{:S(2)}) copy-start(bf16[1024,1024]{1,0:T(8,128)(2,1)} %copy-done.13) | copy-start | bytes 6291460
  184.1 27.4 %collective-permute-start.10 = (bf16[512,1024]{1,0:T(8,128)(2,1)}, bf16[512,1024]{1,0:T(8,128)(2,1)}, u32[]{:S(2)}, u32[]{:S(2)}) collective-permute-start(bf16[512,1024]{1,0:T(8,128)(2,1)} %fusion.13), channel_id=1, source_target_pairs={{8,16},{12,20},{16,8},{20,12},{9,17},{13,21},{17,9},{21,13},{10,18... | collective-permute-start | bytes 3145736 | tf_op jit(solution)/shard_map/ppermute | solution.py:317
  186.3 28.3 %collective-permute-start.9 = (bf16[512,1024]{1,0:T(8,128)(2,1)}, bf16[512,1024]{1,0:T(8,128)(2,1)}, u32[]{:S(2)}, u32[]{:S(2)}) collective-permute-start(bf16[512,1024]{1,0:T(8,128)(2,1)} %fusion.13), channel_id=1, source_target_pairs={{0,8},{4,12},{24,16},{28,20},{1,9},{5,13},{25,17},{29,21},{2,10},{... | collective-permute-start | bytes 3145736 | tf_op jit(solution)/shard_map/ppermute | solution.py:317
  200.1 35.5 %collective-permute-start.15 = (bf16[512,1024]{1,0:T(8,128)(2,1)S(1)}, bf16[512,1024]{1,0:T(8,128)(2,1)}, u32[]{:S(2)}, u32[]{:S(2)}) collective-permute-start(bf16[512,1024]{1,0:T(8,128)(2,1)S(1)} %bitcast.37), channel_id=1, source_target_pairs={{0,8},{4,12},{24,16},{28,20},{1,9},{5,13},{25,17},{29,21},{2,10},{... | collective-permute-start | bytes 3145736 | tf_op jit(solution)/shard_map/ppermute | solution.py:317
  210.3 64.2 %collective-permute-start.14 = (bf16[1024,1024]{1,0:T(8,128)(2,1)S(1)}, bf16[1024,1024]{1,0:T(8,128)(2,1)}, u32[]{:S(2)}, u32[]{:S(2)}) collective-permute-start(bf16[1024,1024]{1,0:T(8,128)(2,1)S(1)} %shard_map.109), channel_id=1, source_target_pairs={{0,4},{4,0},{8,12},{12,8},{16,20},{20,16},{24,28},{28,24},{1,5},{5... | collective-permute-start | bytes 6291464 | tf_op jit(solution)/shard_map/ppermute | solution.py:317
  222.3 76.1 %copy-start.5 = (bf16[3,512,1024]{2,1,0:T(8,128)(2,1)}, bf16[3,512,1024]{2,1,0:T(8,128)(2,1)S(1)}, u32[]{:S(2)}) copy-start(bf16[3,512,1024]{2,1,0:T(8,128)(2,1)S(1)} %shard_map.112) | copy-start | bytes 9437188
  228.5 1.0 copy-start.21
  229.5 6.1 %copy-start.4 = (bf16[3,512,1024]{2,1,0:T(8,128)(2,1)S(1)}, bf16[3,512,1024]{2,1,0:T(8,128)(2,1)}, u32[]{:S(2)}) copy-start(bf16[3,512,1024]{2,1,0:T(8,128)(2,1)} %copy-done.3) | copy-start | bytes 9437188
  229.5 6.1 %copy-start.9 = (bf16[1,512,1024]{2,1,0:T(8,128)(2,1)S(1)}, bf16[1,512,1024]{2,1,0:T(8,128)(2,1)}, u32[]{:S(2)}) copy-start(bf16[1,512,1024]{2,1,0:T(8,128)(2,1)} %copy-done.8) | copy-start | bytes 3145732
  235.6 4.4 %copy-start.23 = (bf16[1024,512]{1,0:T(8,128)(2,1)}, bf16[1024,512]{1,0:T(8,128)(2,1)S(1)}, u32[]{:S(2)}) copy-start(bf16[1024,512]{1,0:T(8,128)(2,1)S(1)} %shard_map.110) | copy-start | bytes 3145732
  240.0 34.5 %collective-permute-start.16 = (bf16[512,1024]{1,0:T(8,128)(2,1)}, bf16[512,1024]{1,0:T(8,128)(2,1)}, u32[]{:S(2)}, u32[]{:S(2)}) collective-permute-start(bf16[512,1024]{1,0:T(8,128)(2,1)} %get-tuple-element.176), channel_id=1, source_target_pairs={{0,8},{4,12},{8,16},{12,20},{16,24},{20,28},{1,9},{5,13},{9,17},{1... | collective-permute-start | bytes 3145736 | tf_op jit(solution)/shard_map/ppermute | solution.py:317
  243.6 30.9 %collective-permute-start.17 = (bf16[512,1024]{1,0:T(8,128)(2,1)}, bf16[512,1024]{1,0:T(8,128)(2,1)}, u32[]{:S(2)}, u32[]{:S(2)}) collective-permute-start(bf16[512,1024]{1,0:T(8,128)(2,1)} %get-tuple-element.175), channel_id=1, source_target_pairs={{8,0},{12,4},{16,8},{20,12},{24,16},{28,20},{9,1},{13,5},{17,9},{2... | collective-permute-start | bytes 3145736 | tf_op jit(solution)/shard_map/ppermute | solution.py:317
  249.4 43.0 %collective-permute-start.21 = (bf16[512,1024]{1,0:T(8,128)(2,1)}, bf16[512,1024]{1,0:T(8,128)(2,1)}, u32[]{:S(2)}, u32[]{:S(2)}) collective-permute-start(bf16[512,1024]{1,0:T(8,128)(2,1)} %fusion.10), channel_id=1, source_target_pairs={{0,8},{4,12},{24,16},{28,20},{1,9},{5,13},{25,17},{29,21},{2,10},{... | collective-permute-start | bytes 3145736 | tf_op jit(solution)/shard_map/ppermute | solution.py:317
  250.7 41.7 %collective-permute-start.22 = (bf16[512,1024]{1,0:T(8,128)(2,1)}, bf16[512,1024]{1,0:T(8,128)(2,1)}, u32[]{:S(2)}, u32[]{:S(2)}) collective-permute-start(bf16[512,1024]{1,0:T(8,128)(2,1)} %fusion.10), channel_id=1, source_target_pairs={{8,16},{12,20},{16,8},{20,12},{9,17},{13,21},{17,9},{21,13},{10,18... | collective-permute-start | bytes 3145736 | tf_op jit(solution)/shard_map/ppermute | solution.py:317
  264.9 1.0 copy-start.10
  265.9 8.6 %copy-start.20 = (bf16[128,1024]{1,0:T(8,128)(2,1)S(1)}, bf16[128,1024]{1,0:T(8,128)(2,1)}, u32[]{:S(2)}) copy-start(bf16[128,1024]{1,0:T(8,128)(2,1)} %copy-done.19) | copy-start | bytes 786436
  274.5 17.8 %copy-start.24 = (bf16[1024,512]{1,0:T(8,128)(2,1)S(1)}, bf16[1024,512]{1,0:T(8,128)(2,1)}, u32[]{:S(2)}) copy-start(bf16[1024,512]{1,0:T(8,128)(2,1)} %copy-done.23) | copy-start | bytes 3145732
  274.5 23.8 %copy-start.22 = (bf16[1024,512]{1,0:T(8,128)(2,1)S(1)}, bf16[1024,512]{1,0:T(8,128)(2,1)}, u32[]{:S(2)}) copy-start(bf16[1024,512]{1,0:T(8,128)(2,1)} %copy-done.21) | copy-start | bytes 3145732
  287.2 11.1 %collective-permute-start.18 = (bf16[128,1024]{1,0:T(8,128)(2,1)S(1)}, bf16[128,1024]{1,0:T(8,128)(2,1)S(1)}, u32[]{:S(2)}, u32[]{:S(2)}) collective-permute-start(bf16[128,1024]{1,0:T(8,128)(2,1)S(1)} %get-tuple-element.134), channel_id=1, source_target_pairs={{4,0},{8,4},{12,8},{16,12},{20,16},{24,20},{28,24},{5,1},{9,5},{13... | collective-permute-start | bytes 786440 | tf_op jit(solution)/shard_map/ppermute | solution.py:317
  292.3 28.6 %collective-permute-start.13 = (bf16[1024,512]{1,0:T(8,128)(2,1)S(1)}, bf16[1024,512]{1,0:T(8,128)(2,1)S(1)}, u32[]{:S(2)}, u32[]{:S(2)}) collective-permute-start(bf16[1024,512]{1,0:T(8,128)(2,1)S(1)} %copy-done.24), channel_id=1, source_target_pairs={{0,4},{4,0},{8,12},{12,8},{16,20},{20,16},{24,28},{28,24},{1,5},{5... | collective-permute-start | bytes 3145736 | tf_op jit(solution)/shard_map/ppermute | solution.py:317
  298.4 43.8 %collective-permute-start.19 = (bf16[1024,512]{1,0:T(8,128)(2,1)S(1)}, bf16[1024,512]{1,0:T(8,128)(2,1)S(1)}, u32[]{:S(2)}, u32[]{:S(2)}) collective-permute-start(bf16[1024,512]{1,0:T(8,128)(2,1)S(1)} %copy-done.22), channel_id=1, source_target_pairs={{0,4},{4,0},{8,12},{12,8},{16,20},{20,16},{24,28},{28,24},{1,5},{5... | collective-permute-start | bytes 3145736 | tf_op jit(solution)/shard_map/ppermute | solution.py:317
  302.4 51.7 %collective-permute-start.23 = (bf16[512,1024]{1,0:T(8,128)(2,1)}, bf16[512,1024]{1,0:T(8,128)(2,1)}, u32[]{:S(2)}, u32[]{:S(2)}) collective-permute-start(bf16[512,1024]{1,0:T(8,128)(2,1)} %get-tuple-element.174), channel_id=1, source_target_pairs={{0,8},{4,12},{8,16},{12,20},{16,24},{20,28},{1,9},{5,13},{9,17},{1... | collective-permute-start | bytes 3145736 | tf_op jit(solution)/shard_map/ppermute | solution.py:317
  305.5 15.3 %copy-start.7 = (bf16[1024,1024]{1,0:T(8,128)(2,1)S(1)}, bf16[1024,1024]{1,0:T(8,128)(2,1)}, u32[]{:S(2)}) copy-start(bf16[1024,1024]{1,0:T(8,128)(2,1)} %copy-done.6) | copy-start | bytes 6291460
  305.5 15.3 %copy-start.11 = (bf16[1024,512]{1,0:T(8,128)(2,1)S(1)}, bf16[1024,512]{1,0:T(8,128)(2,1)}, u32[]{:S(2)}) copy-start(bf16[1024,512]{1,0:T(8,128)(2,1)} %copy-done.10) | copy-start | bytes 3145732
  305.5 48.5 %collective-permute-start.24 = (bf16[512,1024]{1,0:T(8,128)(2,1)}, bf16[512,1024]{1,0:T(8,128)(2,1)}, u32[]{:S(2)}, u32[]{:S(2)}) collective-permute-start(bf16[512,1024]{1,0:T(8,128)(2,1)} %get-tuple-element.173), channel_id=1, source_target_pairs={{8,0},{12,4},{16,8},{20,12},{24,16},{28,20},{9,1},{13,5},{17,9},{2... | collective-permute-start | bytes 3145736 | tf_op jit(solution)/shard_map/ppermute | solution.py:317
  328.3 34.1 %collective-permute-start.25 = (bf16[128,512]{1,0:T(8,128)(2,1)}, bf16[128,512]{1,0:T(8,128)(2,1)S(1)}, u32[]{:S(2)}, u32[]{:S(2)}) collective-permute-start(bf16[128,512]{1,0:T(8,128)(2,1)} %get-tuple-element.142), channel_id=1, source_target_pairs={{4,0},{8,4},{12,8},{16,12},{20,16},{24,20},{28,24},{5,1},{9,5},{13... | collective-permute-start | bytes 393224 | tf_op jit(solution)/shard_map/ppermute | solution.py:317
  349.7 11.2 %copy-start.17 = (bf16[1024,512]{1,0:T(8,128)(2,1)}, bf16[1024,512]{1,0:T(8,128)(2,1)S(1)}, u32[]{:S(2)}) copy-start(bf16[1024,512]{1,0:T(8,128)(2,1)S(1)} %get-tuple-element.150.gm) | copy-start | bytes 3145732
  349.7 20.6 %collective-permute-start.20 = (bf16[128,512]{1,0:T(8,128)(2,1)}, bf16[128,512]{1,0:T(8,128)(2,1)S(1)}, u32[]{:S(2)}, u32[]{:S(2)}) collective-permute-start(bf16[128,512]{1,0:T(8,128)(2,1)} %get-tuple-element.151), channel_id=1, source_target_pairs={{4,0},{8,4},{12,8},{16,12},{20,16},{24,20},{28,24},{5,1},{9,5},{13... | collective-permute-start | bytes 393224 | tf_op jit(solution)/shard_map/ppermute | solution.py:317
  355.0 14.7 %all-to-all-start = ((f32[8,16,128]{2,1,0:T(8,128)}), f32[8,16,128]{2,1,0:T(8,128)S(1)}, u32[]{:S(2)}, u32[]{:S(2)}) async-start(f32[8,16,128]{2,1,0:T(8,128)} %bitcast.21), calls=%async_computation | async-start | bytes 131072 | tf_op jit(solution)/shard_map/all_to_all | solution.py:508
  358.3 2.6 copy-start.25
  360.9 2.9 copy-start
  362.4 7.9 %copy-start.18 = (bf16[1024,512]{1,0:T(8,128)(2,1)S(1)}, bf16[1024,512]{1,0:T(8,128)(2,1)}, u32[]{:S(2)}) copy-start(bf16[1024,512]{1,0:T(8,128)(2,1)} %copy-done.17) | copy-start | bytes 3145732
  370.3 2.2 copy-start.1
Sparse Core Ops, SparseCore 0:
  12.0 34.6 all-gather.4
  100.1 33.7 all-gather.6
where the time goes:
time: 388 us; the launch traced here: 385 us
  Pallas kernels  161 us (41%)
  waiting for transfers between devices  99 us (26%)
  starting transfers between devices  68.2 us (18%)
  other arithmetic  25.4 us (7%)
  local copies, waits for them, and re-layouts  16.7 us (4%)
  between operations  14.7 us (4%)
    ppermute x26, waiting for transfers between devices, send(): return lax.ppermute(x, 'seq', pairs)  99 us
    ppermute x26, starting transfers between devices, send(): return lax.ppermute(x, 'seq', pairs)  64.8 us
    pallas_call x6, Pallas kernels, gate_grad(): pl.pallas_call(gate_kernel, grid_spec=pltpu.PrefetchScalarGridSpec(num_sc...  40.9 us
    pallas_call x6, Pallas kernels, weight_rows(): pl.pallas_call(functools.partial(rows_kernel, n), grid_spec=pltpu.Prefetc...  40.2 us
    pallas_call x3, Pallas kernels, middle(): pl.pallas_call(kernel, grid=(tiles,), in_specs=in_specs, out_specs=[here,...  27.6 us
    pallas_call x3, Pallas kernels, backward(): pl.pallas_call(backward_kernel, grid=(tiles,), in_specs=in_specs, out_spe...  22.1 us
    pallas_call x2, Pallas kernels, forward(): pl.pallas_call(forward_kernel, grid=(tiles,), in_specs=[here, here, here,...  19.8 us
    unnamed x54, local copies, waits for them, and re-layouts  12.5 us
  transfers between devices with their start and end apart: 29, of which 7 were waited for; matrix products, arithmetic and copies ran while one was open for 7% of the time, Pallas kernels for 40%

commit v1 on v0

--- a/solution.py
+++ b/solution.py
@@ -108,7 +108,7 @@
             here,
             here,
             here,
-            pl.BlockSpec((FILT, LANES), lambda i: (0, i)),
+            pl.BlockSpec((FILT, LANES), lambda i: (0, chunk * tiles + i)),
             pl.BlockSpec((GPT * FILT, 2 * FILT), lambda i: (chunk * tiles + i, 0)),
         ],
         out_specs=[out, out],
@@ -163,7 +163,7 @@
     args = [own, *others, q, k, v, mixed, prior]
     in_specs = [part] * (1 + n_other) + [here] * 3
     in_specs.append(pl.BlockSpec((rows, LANES), lambda i: (0, local // LANES + i)))
-    in_specs.append(pl.BlockSpec((FILT, LANES), lambda i: (0, local // LANES + i)))
+    in_specs.append(pl.BlockSpec((FILT, LANES), lambda i: (0, first // LANES + i)))
     aliases = {}
     if filled is not None:
         aliases = {len(args): 0}
@@ -266,42 +266,135 @@
     )(pick, *([cot] * LINE), *weights)
 
 
-def rows_kernel(n, pick, *refs):
+def rows_kernel(n, halves, pick, *refs):
     out = refs[-1]
-    cot, gated = refs[0][0], refs[n][...]
+    cot = refs[0][0]
     if n > 1:
         cot = jnp.concatenate([ref[0] for ref in refs[:n]], axis=0)
-        gated = jnp.concatenate([ref[...] for ref in refs[n : 2 * n]], axis=0)
-    total = lax.dot_general(cot, gated, (((0,), (0,)), ((), ())), preferred_element_type=F32)
-    if len(refs) > 2 * n + 1:
-        total = total + refs[2 * n][0]
-    out[0] = total.astype(out.dtype)
-
-
-def weight_rows(pick, cots, gateds, dtype, base=None, skip=0):
+
+    def write(gated_refs):
+        gated = gated_refs[0][...]
+        if n > 1:
+            gated = jnp.concatenate([ref[...] for ref in gated_refs], axis=0)
+        total = lax.dot_general(cot, gated, (((0,), (0,)), ((), ())), preferred_element_type=F32)
+        if len(refs) > n + n * halves + 1:
+            total = total + refs[-2][0]
+        out[0] = total.astype(out.dtype)
+
+    for h in range(halves):
+        pl.when(pl.program_id(1) == h)(
+            functools.partial(write, refs[n + n * h : n + n * (h + 1)])
+        )
+
+
+def weight_rows(pick, cots, gateds, dtype, base=None, skip=0, lead=0):
     _, rows, depth = cots[0].shape
-    width = gateds[0].shape[1]
+    width = gateds[0][0].shape[1]
     blocks = pick.shape[0]
-    tile = width if blocks > 1 else min(512, width)
-    n = len(cots)
+    n, halves = len(cots), len(gateds)
     in_specs = [pl.BlockSpec((1, rows, depth), lambda j, i, pick: (pick[j], 0, 0))] * n
-    in_specs += [pl.BlockSpec((rows, tile), lambda j, i, pick: (0, i))] * n
-    args = [*cots, *gateds]
+    in_specs += [pl.BlockSpec((rows, width), lambda j, i, pick: (0, 0))] * (n * halves)
+    args = [*cots, *(x for half in gateds for x in half)]
     if base is not None:
-        in_specs.append(pl.BlockSpec((1, depth, tile), lambda j, i, pick: (j + skip, 0, i)))
+        in_specs.append(
+            pl.BlockSpec((1, depth, width), lambda j, i, pick: (j + skip, 0, lead + i))
+        )
         args.append(base)
     return pl.pallas_call(
-        functools.partial(rows_kernel, n),
+        functools.partial(rows_kernel, n, halves),
         grid_spec=pltpu.PrefetchScalarGridSpec(
             num_scalar_prefetch=1,
-            grid=(blocks, width // tile),
+            grid=(blocks, halves),
             in_specs=in_specs,
-            out_specs=pl.BlockSpec((1, depth, tile), lambda j, i, pick: (j, 0, i)),
+            out_specs=pl.BlockSpec((1, depth, width), lambda j, i, pick: (j, 0, i)),
         ),
-        out_shape=jax.ShapeDtypeStruct((blocks, depth, width), dtype),
+        out_shape=jax.ShapeDtypeStruct((blocks, depth, halves * width), dtype),
         compiler_params=params(),
         cost_estimate=cost(2 * n * rows * depth * width, 2 * n * rows * (depth + width)),
     )(pick, *args)
+
+
+def second_kernel(halves, rows_ref, *refs):
+    out = refs[-1]
+
+    def write(came):
+        out[...] = (rows_ref[0].astype(F32) + came[...].astype(F32)).astype(out.dtype)
+
+    for h in range(halves):
+        pl.when(pl.program_id(0) == h)(functools.partial(write, refs[h]))
+
+
+def second_sums(rows, came):
+    _, depth, width = rows.shape
+    halves = len(came)
+    cols = width // halves
+    return pl.pallas_call(
+        functools.partial(second_kernel, halves),
+        grid=(halves, 2),
+        in_specs=[pl.BlockSpec((1, depth // 2, cols), lambda h, i: (0, i, h))]
+        + [pl.BlockSpec((depth // 2, cols), lambda h, i: (i, 0))] * halves,
+        out_specs=pl.BlockSpec((depth // 2, cols), lambda h, i: (i, h)),
+        out_shape=jax.ShapeDtypeStruct((depth, width), BF16),
+        compiler_params=params(),
+        cost_estimate=cost(depth * width, 6 * depth * width),
+    )(rows, *came)
+
+
+def third_kernel(halves, at, rows_ref, outer_ref, inner_ref, *refs):
+    up_out, down_out = refs[halves:]
+    mine = rows_ref[0].astype(F32)
+    outer, inner = outer_ref[...].astype(F32), inner_ref[...].astype(F32)
+    add_up = jnp.where(at[0] == 1, outer, inner)
+    add_down = jnp.where(at[0] == 1, inner, outer)
+
+    def write(first):
+        other = first[...].astype(F32)
+        up_out[...] = (jnp.where(at[1] == 1, other, mine) + add_up).astype(BF16)
+        down_out[...] = (jnp.where(at[0] == 1, other, mine) + add_down).astype(BF16)
+
+    for h in range(halves):
+        pl.when(pl.program_id(0) == h)(functools.partial(write, refs[h]))
+
+
+def third_sums(at, rows, outer, inner, first):
+    _, depth, width = rows.shape
+    halves = len(first)
+    cols = width // halves
+    whole = pl.BlockSpec((depth // 2, cols), lambda h, i, at: (i, h))
+    shape = jax.ShapeDtypeStruct((depth, width), BF16)
+    return pl.pallas_call(
+        functools.partial(third_kernel, halves),
+        grid_spec=pltpu.PrefetchScalarGridSpec(
+            num_scalar_prefetch=1,
+            grid=(halves, 2),
+            in_specs=[pl.BlockSpec((1, depth // 2, cols), lambda h, i, at: (1, i, h)), whole, whole]
+            + [pl.BlockSpec((depth // 2, cols), lambda h, i, at: (i, 0))] * halves,
+            out_specs=[whole, whole],
+        ),
+        out_shape=[shape, shape],
+        compiler_params=params(),
+        cost_estimate=cost(4 * depth * width, 12 * depth * width),
+    )(at, rows, outer, inner, *first)
+
+
+def last_kernel(rows_ref, below, above, out):
+    total = rows_ref[0].astype(F32) + below[...].astype(F32) + above[...].astype(F32)
+    out[...] = total.astype(out.dtype)
+
+
+def last_sums(rows, below, above):
+    _, depth, width = rows.shape
+    tile = depth // 4
+    whole = pl.BlockSpec((tile, width), lambda i: (i, 0))
+    return pl.pallas_call(
+        last_kernel,
+        grid=(4,),
+        in_specs=[pl.BlockSpec((1, tile, width), lambda i: (2, i, 0)), whole, whole],
+        out_specs=whole,
+        out_shape=jax.ShapeDtypeStruct((depth, width), BF16),
+        compiler_params=params(),
+        cost_estimate=cost(2 * depth * width, 8 * depth * width),
+    )(rows, below, above)
 
 
 def shards(seq, ch, queries, keys, values, filters, grad_out, out_weight):
@@ -354,32 +447,19 @@
         ]
     ).astype(jnp.int32)
 
-    def rows_own(h):
-        return weight_rows(jnp.concatenate([first_pick, rest_pick]), cots[:1], [gateds[h]], F32)
+    places = jnp.stack([z == 1, z == 2]).astype(jnp.int32)
 
     def rows_first(h):
-        return weight_rows(first_pick, cots[1:], got[h], BF16, base[h])[0]
-
-    def rows_rest(h):
-        return weight_rows(rest_pick, cots[1:], got[h], BF16, base[h], 1)
+        return weight_rows(first_pick, cots[1:], got[h : h + 1], BF16, base, 0, h)[0]
 
     def send_first(x):
         return along_line(x, [(0, 1), (3, 2)])
 
-    def send_second(h, came):
-        x = (rest[h][0].astype(F32) + came.astype(F32)).astype(BF16)
+    def send_second(x):
         return along_line(x, [(0, 1), (3, 2)]), along_line(x, [(1, 2), (2, 1)])
 
-    def send_third(h, outer_in, inner_in):
-        mine, other = rest[h][1].astype(F32), first[h].astype(F32)
-        outer_in, inner_in = outer_in.astype(F32), inner_in.astype(F32)
-        up = jnp.where(z == 2, other, mine) + jnp.where(z == 1, outer_in, inner_in)
-        down = jnp.where(z == 1, other, mine) + jnp.where(z == 1, inner_in, outer_in)
-        return along_line(up.astype(BF16), up_pairs), along_line(down.astype(BF16), down_pairs)
-
-    def last_sum(h):
-        below, above = sums[h]
-        return (rest[h][2].astype(F32) + below.astype(F32) + above.astype(F32)).astype(BF16)
+    def send_third(up, down):
+        return along_line(up, up_pairs), along_line(down, down_pairs)
 
     def shares(span):
         return [gate_grad(pick, cots[r], weights, span) for r in range(1, inner)]
@@ -387,20 +467,14 @@
     def send_shares(parts):
         return [around_inner(part, inner - r) for r, part in enumerate(parts, 1)]
 
-    gateds, mixeds, got, sums, first, rest, base = ([None] * chunks for _ in range(7))
+    gateds, mixeds, got, sums, first = ([None] * chunks for _ in range(5))
     later_halves = list(each[1:])
-    spans = [(0, 0, cols, 0)]
-    for h in later_halves:
-        spans += [(h, lo, cols // 2, h * cols + lo) for lo in (0, cols // 2)]
-    parts, others, owns, gms, laters, taps = ([None] * len(spans) for _ in range(6))
-
-    priors = []
-    for h in each:
-        tail = (slice(rows - FILT, rows), slice(h * cols, (h + 1) * cols))
-        priors.append(product_of(keys[tail], values[tail]))
-    cot_here = after(grad_out, *priors)
-    next_pairs = [(i, i + 1) for i in range(seq - 1)]
-    priors[0] = send(priors[0], next_pairs)
+    spans = [(h, 0, cols, h * cols) for h in each]
+    parts, others, gms, laters, taps = ([None] * chunks for _ in range(5))
+
+    prior = product_of(keys[rows - FILT :], values[rows - FILT :])
+    cot_here = after(grad_out, prior)
+    prior = send(prior, [(i, i + 1) for i in range(seq - 1)])
     paired = inner == 2 and ch == LINE
     other = cot_here
     cots = []
@@ -409,19 +483,13 @@
         other = lax.dynamic_slice(cot_here, (0, (1 - y) * depth), (rows, depth))
         cots = [lax.all_gather(kept, "ch", axis=0, tiled=False)]
     back, ahead = tables(filters)
-    priors, other, weight = fence(priors, other, out_weight)
-    for h in later_halves:
-        priors[h] = send(priors[h], next_pairs)
+    prior, other, weight = fence(prior, other, out_weight)
 
     up1, down1 = along_line(weight, up_pairs), along_line(weight, down_pairs)
     swapped = around_inner(other, 1) if paired else other
     for h in each:
-        gateds[h], mixeds[h] = forward(queries, keys, values, priors[h], back, h, chunks)
-    if paired:
-        base[0] = rows_own(0)
-    up1, down1, swapped, gateds, cots, priors, base = fence(
-        up1, down1, swapped, gateds, cots, priors, base
-    )
+        gateds[h], mixeds[h] = forward(queries, keys, values, prior, back, h, chunks)
+    up1, down1, swapped, gateds, cots, prior = fence(up1, down1, swapped, gateds, cots, prior)
 
     up2 = along_line(up1, [(1, 2), (2, 3)])
     down2 = along_line(down1, [(2, 1), (1, 0)])
@@ -433,76 +501,57 @@
         for shift in range(inner):
             part = lax.dynamic_index_in_dim(full, (y + shift) % inner, 0, keepdims=False)
             cots.append(part if shift == 0 else around_inner(part, shift))
-        base[0] = rows_own(0)
     for h in each:
         got[h] = swap_gated(h)
-
-    got[0], cots, gateds, base = fence(got[0], cots, gateds, base)
+    all_pick = jnp.concatenate([first_pick, rest_pick])
+    base = weight_rows(all_pick, cots[:1], [[x] for x in gateds], F32)
+
+    got[0], cots, base = fence(got[0], cots, base)
     first[0] = rows_first(0)
     sums[0] = send_first(first[0])
     up2, down2, first[0] = fence(up2, down2, first[0])
 
     second = merge(up2, down2)
     third = along_line(second, [(2, 3), (1, 0)])
-    rest[0] = rows_rest(0)
-    sums[0], rest[0], gateds = fence(sums[0], rest[0], gateds)
-    sums[0] = send_second(0, sums[0])
-    for h in later_halves:
-        base[h] = rows_own(h)
-    got[1:], base = fence(got[1:], base)
-
+    got, second, sums[0] = fence(got, second, sums[0])
     for h in later_halves:
         first[h] = rows_first(h)
         sums[h] = send_first(first[h])
     third, first = fence(third, first)
+
     weights = [weight, up1, down1, second, third]
     parts[0] = shares(spans[0])
     others[0] = send_shares(parts[0])
-
-    sums[0], parts[0], third, base = fence(sums[0], parts[0], third, base)
-    sums[0] = send_third(0, *sums[0])
+    parts[0], got, third = fence(parts[0], got, third)
+    rest = weight_rows(rest_pick, cots[1:], got, BF16, base, 1)
+    rest, third = fence(rest, third)
+    weights = [weight, up1, down1, second, third]
     for h in later_halves:
-        rest[h] = rows_rest(h)
-    weights = [weight, up1, down1, second, third]
-    for n, span in enumerate(spans[1:], 1):
-        parts[n] = shares(span)
-    for n in range(1, len(spans), 2):
-        others[n] = send_shares(parts[n])
-    sums[1:], parts, rest = fence(sums[1:], parts, rest)
-    for h in later_halves:
-        sums[h] = send_second(h, sums[h])
-    third, _ = fence(third, parts)
+        parts[h] = shares(spans[h])
+        others[h] = send_shares(parts[h])
+    sums, rest, parts, third = fence(sums, rest, parts, third)
+    sums = send_second(second_sums(rest, sums))
     weights = [weight, up1, down1, second, third]
     owns = [gate_grad(pick, cots[0], weights, span) for span in spans]
-    others[0], owns, sums[0] = fence(others[0], owns, sums[0])
+    others[0], owns = fence(others[0], owns)
 
     grad_queries = None
     grad_kv = None
     back_pairs = [(i + 1, i) for i in range(seq - 1)]
-    done = []
-    for n, span in enumerate(spans):
-        half = span[0]
-        grad_queries, gms[n], edge, taps[n] = middle(
-            owns[n], others[n], queries, keys, values, mixeds[half], priors[half], grad_queries, span
+    for h, span in enumerate(spans):
+        grad_queries, gms[h], edge, taps[h] = middle(
+            owns[h], others[h], queries, keys, values, mixeds[h], prior, grad_queries, span
         )
-        laters[n] = send(edge, back_pairs)
-        if n == 0:
-            for m in range(2, len(spans), 2):
-                others[m] = send_shares(after(parts[m], laters[0]))
-            for g in later_halves:
-                sums[g] = send_third(g, *after(sums[g], laters[0]))
-            done.append(last_sum(0))
-            others[1:2], owns, done = fence(others[1:2], owns, done)
-        if n == 1:
-            gms[0], _ = fence(gms[0], edge)
-            grad_kv = backward(gms[0], laters[0], keys, values, ahead, grad_kv, spans[0])
-            others[2:], grad_kv = fence(others[2:], grad_kv)
-    for h in later_halves:
-        sums[h], gms[1], _ = fence(sums[h], gms[1], edge)
-        done.append(last_sum(h))
-    for n in range(1 if len(spans) > 1 else 0, len(spans)):
-        grad_kv = backward(gms[n], laters[n], keys, values, ahead, grad_kv, spans[n])
-    grad_weight = jnp.concatenate(done, axis=1)
+        laters[h] = send(edge, back_pairs)
+        if h == 0:
+            sums = send_third(*third_sums(places, rest, *after(sums, edge), first))
+            others, owns, edge = fence(others, owns, edge)
+    gms, _ = fence(gms, edge)
+    for h, span in enumerate(spans):
+        grad_kv = backward(gms[h], laters[h], keys, values, ahead, grad_kv, span)
+        if h == 0:
+            sums, grad_kv = fence(sums, grad_kv)
+    grad_weight = last_sums(rest, *sums)
     taps = jnp.concatenate(taps, axis=0)[:, 1 : FILT + 1][:, ::-1]
     taps = taps.T.reshape(seq, FILT // seq, -1)
     taps = jnp.sum(lax.all_to_all(taps, "seq", 0, 0), axis=0)

time: 388 us -> 367 us (0.946)
  other arithmetic: 25.4 us -> 5.83 us
  starting transfers between devices: 68.2 us -> 53.5 us
  waiting for transfers between devices: 99 us -> 106 us
  Pallas kernels: 161 us -> 167 us
    all_to_all x1, waiting for transfers between devices: 0.01 us -> 23.7 us  [shards(): taps = jnp.sum(lax.all_to_all(taps, 'seq', 0, 0), axis=0)]
    convert_element_type x6 -> x1, other arithmetic: 18.1 us -> 0.07 us  [shards(): places = jnp.stack([z == 1, z == 2]).astype(jnp.int32)]
    ppermute x26 -> x19, starting transfers between devices: 64.8 us -> 47.2 us  [send(): return lax.ppermute(x, 'seq', pairs)]
    ppermute x26 -> x19, waiting for transfers between devices: 99 us -> 82.2 us  [send(): return lax.ppermute(x, 'seq', pairs)]
    pallas_call x6 -> x7, Pallas kernels: 40.2 us -> 55 us  [the longest x4 39.5 us: weight_rows(): pl.pallas_call(functools.partial(rows_kernel, n, halves), grid_spec=pltpu...]
    pallas_call x6 -> x4, Pallas kernels: 40.9 us -> 34.3 us  [gate_grad(): pl.pallas_call(gate_kernel, grid_spec=pltpu.PrefetchScalarGridSpec(num_sc...]
    pallas_call x3 -> x2, Pallas kernels: 27.6 us -> 25.8 us  [middle(): pl.pallas_call(kernel, grid=(tiles,), in_specs=in_specs, out_specs=[here,...]
    pallas_call x3 -> x2, Pallas kernels: 22.1 us -> 20.9 us  [backward(): pl.pallas_call(backward_kernel, grid=(tiles,), in_specs=in_specs, out_spe...]
  transfers between devices with their start and end apart: 29 -> 22, of which waited for: 7 -> 9; matrix products, arithmetic and copies ran while one was open for 7% -> 2% of each run, Pallas kernels for 40% -> 43%
where the time goes in v1:
time: 367 us; the launch traced here: 363 us
  Pallas kernels  167 us (46%)
  waiting for transfers between devices  106 us (29%)
  starting transfers between devices  53.5 us (15%)
  local copies, waits for them, and re-layouts  16.4 us (4%)
  between operations  14.4 us (4%)
  other arithmetic  5.83 us (2%)
    ppermute x19, waiting for transfers between devices, send(): return lax.ppermute(x, 'seq', pairs)  82.2 us
    ppermute x19, starting transfers between devices, send(): return lax.ppermute(x, 'seq', pairs)  47.2 us
    pallas_call x4, Pallas kernels, weight_rows(): pl.pallas_call(functools.partial(rows_kernel, n, halves), grid_spec=pltpu...  39.5 us
    pallas_call x4, Pallas kernels, gate_grad(): pl.pallas_call(gate_kernel, grid_spec=pltpu.PrefetchScalarGridSpec(num_sc...  34.3 us
    pallas_call x2, Pallas kernels, middle(): pl.pallas_call(kernel, grid=(tiles,), in_specs=in_specs, out_specs=[here,...  25.8 us
    all_to_all x1, waiting for transfers between devices, shards(): taps = jnp.sum(lax.all_to_all(taps, 'seq', 0, 0), axis=0)  23.7 us
    pallas_call x2, Pallas kernels, backward(): pl.pallas_call(backward_kernel, grid=(tiles,), in_specs=in_specs, out_spe...  20.9 us
    pallas_call x2, Pallas kernels, forward(): pl.pallas_call(forward_kernel, grid=(tiles,), in_specs=[here, here, here,...  19.8 us
  transfers between devices with their start and end apart: 22, of which 9 were waited for; matrix products, arithmetic and copies ran while one was open for 2% of the time, Pallas kernels for 43%

profile of v1, /device:TPU:10, one launch (start us, length us, event | category | flops | bytes accessed | tf_op | source)
XLA Modules:
  0.0 362.9 jit_solution(2905805636946274419)
XLA Ops:
  7.2 1.3 multiply_convert_fusion
  8.6 3.1 constant_dynamic-slice_fusion
  11.8 3.4 collective-permute-start
  15.3 13.0 %collective-permute-done.prior.refs_5_ = bf16[128,2048]{1,0:T(8,128)(2,1)S(1)} collective-permute-done((bf16[128,2048]{1,0:T(8,128)(2,1)S(1)}, bf16[128,2048]{1,0:T(8,128)(2,1)S(1)}, u32[]{:S(2)}, u32[]{:S(2)}) %collective-permute-start) | collective-permute-done | bytes 524320 | tf_op jit(solution)/shard_map/ppermute | solution.py:410
  28.3 3.5 collective-permute-start.1
  31.8 3.7 %collective-permute-start.2 = (bf16[512,2048]{1,0:T(8,128)(2,1)S(1)}, bf16[512,2048]{1,0:T(8,128)(2,1)}, u32[]{:S(2)}, u32[]{:S(2)}) collective-permute-start(bf16[512,2048]{1,0:T(8,128)(2,1)S(1)} %copy-done), channel_id=1, source_target_pairs={{8,0},{12,4},{16,8},{20,12},{24,16},{28,20},{9,1},{13,5},{17,9},{2... | collective-permute-start | bytes 6291464 | tf_op jit(solution)/shard_map/ppermute | solution.py:410
  35.5 0.7 collective-permute-start.3
  36.2 0.1 rev.6
  36.4 0.1 maximum_maximum_fusion.back_ref
  36.5 11.0 %shard_map.101 = (bf16[16384,256]{1,0:T(8,128)(2,1)}, bf16[16384,256]{1,0:T(8,128)(2,1)}) custom-call(f32[128,256]{1,0:T(8,128)S(1)} %maximum_maximum_fusion.back_ref, f32[128,256]{1,0:T(8,128)S(1)} %concatenate.14.ahead_ref), custom_call_target="tpu_custom_call" | custom-call | flops 524288 | bytes 262144 | tf_op jit(solution)/shard_map/pallas_call | solution.py:54
  47.4 9.9 %shard_map.102 = (bf16[1024,1024]{1,0:T(8,128)(2,1)S(1)}, bf16[1024,1024]{1,0:T(8,128)(2,1)S(1)}) custom-call(bf16[1024,2048]{1,0:T(8,128)(2,1)} %refs_1_.3, bf16[1024,2048]{1,0:T(8,128)(2,1)} %k.7, bf16[1024,2048]{1,0:T(8,128)(2,1)} %v.7, bf16[128,2048]{1,0:T(8,128)(2,1)S(1)} %collective-permute-done.prior.refs_5_, bf16[16384,256]{1,0:T(8,128)(2,1)} %get-tuple-element.76.table), custom_call_target="tpu_custom_call" | custom-call | flops 67108864 | bytes 229376 | tf_op jit(solution)/shard_map/pallas_call | solution.py:104
  57.3 1.3 copy-done.4
  58.7 1.3 copy-done.7
  60.0 9.9 %shard_map.103 = (bf16[1024,1024]{1,0:T(8,128)(2,1)S(1)}, bf16[1024,1024]{1,0:T(8,128)(2,1)S(1)}) custom-call(bf16[1024,2048]{1,0:T(8,128)(2,1)} %refs_1_.3, bf16[1024,2048]{1,0:T(8,128)(2,1)} %k.7, bf16[1024,2048]{1,0:T(8,128)(2,1)} %v.7, bf16[128,2048]{1,0:T(8,128)(2,1)S(1)} %collective-permute-done.prior.refs_5_, bf16[16384,256]{1,0:T(8,128)(2,1)} %get-tuple-element.76.table), custom_call_target="tpu_custom_call" | custom-call | flops 67108864 | bytes 229376 | tf_op jit(solution)/shard_map/pallas_call | solution.py:104
  69.9 1.3 copy-done.3
  71.2 1.3 copy-done.5
  72.5 4.3 %collective-permute-done.1.refs_5_ = bf16[512,2048]{1,0:T(8,128)(2,1)} collective-permute-done((bf16[512,2048]{1,0:T(8,128)(2,1)S(1)}, bf16[512,2048]{1,0:T(8,128)(2,1)}, u32[]{:S(2)}, u32[]{:S(2)}) %collective-permute-start.1) | collective-permute-done | bytes 2097184 | tf_op jit(solution)/shard_map/ppermute | solution.py:410
  76.8 3.2 collective-permute-done.2.refs_6_
  80.0 0.8 collective-permute-start.4
  80.8 4.9 %collective-permute-start.6 = (bf16[512,2048]{1,0:T(8,128)(2,1)}, bf16[512,2048]{1,0:T(8,128)(2,1)}, u32[]{:S(2)}, u32[]{:S(2)}) collective-permute-start(bf16[512,2048]{1,0:T(8,128)(2,1)} %collective-permute-done.1.refs_5_), channel_id=1, source_target_pairs={{8,16},{12,20},{16,24},{20,28},{9,17},{13,21},{17,25},{21,29},{10,... | collective-permute-start | bytes 6291464 | tf_op jit(solution)/shard_map/ppermute | solution.py:410
  85.7 1.9 collective-permute-start.7
  87.6 1.4 collective-permute-start.5
  89.0 1.7 copy-done.6
  90.7 1.6 copy-done.8
  92.3 16.0 %shard_map.104.refs_2_.refs_3_ = f32[4,512,2048]{2,1,0:T(8,128)} custom-call(s32[4]{0:T(128)S(1)} %pad_add_fusion.pick, bf16[4,1024,512]{2,1,0:T(8,128)(2,1)} %bitcast.32, bf16[1024,1024]{1,0:T(8,128)(2,1)S(1)} %copy-done.8, bf16[1024,1024]{1,0:T(8,128)(2,1)S(1)} %copy-done.6), custom_call_target="tpu_custom_call" | custom-call | flops 16777216 | bytes 49152 | tf_op jit(solution)/shard_map/pallas_call | solution.py:303
  108.3 20.6 %collective-permute-done.4.refs_1_ = bf16[1024,1024]{1,0:T(8,128)(2,1)} collective-permute-done((bf16[1024,1024]{1,0:T(8,128)(2,1)}, bf16[1024,1024]{1,0:T(8,128)(2,1)}, u32[]{:S(2)}, u32[]{:S(2)}) %collective-permute-start.4) | collective-permute-done | bytes 2097184 | tf_op jit(solution)/shard_map/ppermute | solution.py:410
  129.0 3.8 %shard_map.105 = bf16[1,512,1024]{2,1,0:T(8,128)(2,1)S(1)} custom-call(s32[1]{0:T(128)} %bitcast.8.pick, bf16[4,1024,512]{2,1,0:T(8,128)(2,1)} %bitcast.21, bf16[1024,1024]{1,0:T(8,128)(2,1)} %collective-permute-done.4.refs_1_, f32[4,512,2048]{2,1,0:T(8,128)} %shard_map.104.refs_2_.refs_3_), custom_call_target="tpu_custom_call" | custom-call | flops 16777216 | bytes 49152 | tf_op jit(solution)/shard_map/pallas_call | solution.py:303
  132.8 3.5 broadcast_select_fusion.refs_7_
  136.3 5.1 %collective-permute-start.9 = (bf16[512,2048]{1,0:T(8,128)(2,1)}, bf16[512,2048]{1,0:T(8,128)(2,1)}, u32[]{:S(2)}, u32[]{:S(2)}) collective-permute-start(bf16[512,2048]{1,0:T(8,128)(2,1)} %broadcast_select_fusion.refs_7_), channel_id=1, source_target_pairs={{16,24},{20,28},{8,0},{12,4},{17,25},{21,29},{9,1},{13,5},{18,26},... | collective-permute-start | bytes 6291464 | tf_op jit(solution)/shard_map/ppermute | solution.py:410
  141.4 1.3 collective-permute-start.8
  142.7 27.9 %collective-permute-done.5.refs_1_.refs_2_ = bf16[1024,1024]{1,0:T(8,128)(2,1)} collective-permute-done((bf16[1024,1024]{1,0:T(8,128)(2,1)}, bf16[1024,1024]{1,0:T(8,128)(2,1)}, u32[]{:S(2)}, u32[]{:S(2)}) %collective-permute-start.5) | collective-permute-done | bytes 2097184 | tf_op jit(solution)/shard_map/ppermute | solution.py:410
  170.6 1.0 copy-done.11
  171.6 4.8 %shard_map.106 = bf16[1,512,1024]{2,1,0:T(8,128)(2,1)} custom-call(s32[1]{0:T(128)} %bitcast.8.pick, bf16[4,1024,512]{2,1,0:T(8,128)(2,1)} %bitcast.22, bf16[1024,1024]{1,0:T(8,128)(2,1)} %collective-permute-done.5.refs_1_.refs_2_, f32[4,512,2048]{2,1,0:T(8,128)} %shard_map.104.refs_2_.refs_3_), custom_call_target="tpu_custom_call" | custom-call | flops 16777216 | bytes 49152 | tf_op jit(solution)/shard_map/pallas_call | solution.py:303
  176.4 1.3 collective-permute-start.11
  177.7 0.1 stack.46.pick
  177.9 2.2 collective-permute-done.9.refs_8_
  180.0 8.6 %shard_map.107 = bf16[1024,1024]{1,0:T(8,128)(2,1)S(1)} custom-call(s32[6]{0:T(128)S(1)} %stack.46.pick, bf16[4,1024,512]{2,1,0:T(8,128)(2,1)} %bitcast.23, bf16[4,1024,512]{2,1,0:T(8,128)(2,1)} %bitcast.24, bf16[4,1024,512]{2,1,0:T(8,128)(2,1)} %bitcast.25, bf16[4,1024,512]{2,1,0:T(8,128)(2,1)} %bitcast.26, bf16[512,2048]{1,0:T(8,128)(2,1)S(1)} %copy-done, ...), custom_call_target="tpu_custom_call" | custom-call | flops 67108864 | bytes 163840 | tf_op jit(solution)/shard_map/pallas_call | solution.py:252
  188.6 1.2 collective-permute-start.10
  189.8 14.8 %shard_map.108.rows_ref = bf16[3,512,2048]{2,1,0:T(8,128)(2,1)} custom-call(s32[3]{0:T(128)S(1)} %pad_add_fusion.1.pick, bf16[4,1024,512]{2,1,0:T(8,128)(2,1)} %bitcast.27, bf16[1024,1024]{1,0:T(8,128)(2,1)} %collective-permute-done.4.refs_1_, bf16[1024,1024]{1,0:T(8,128)(2,1)} %collective-permute-done.5.refs_1_.refs_2_, ...), custom_call_target="tpu_custom_call" | custom-call | flops 16777216 | bytes 49152 | tf_op jit(solution)/shard_map/pallas_call | solution.py:303
  204.6 8.6 %shard_map.109 = bf16[1024,1024]{1,0:T(8,128)(2,1)S(1)} custom-call(s32[6]{0:T(128)S(1)} %stack.46.pick, bf16[4,1024,512]{2,1,0:T(8,128)(2,1)} %bitcast.28, bf16[4,1024,512]{2,1,0:T(8,128)(2,1)} %bitcast.29, bf16[4,1024,512]{2,1,0:T(8,128)(2,1)} %bitcast.30, bf16[4,1024,512]{2,1,0:T(8,128)(2,1)} %bitcast.31, bf16[512,2048]{1,0:T(8,128)(2,1)S(1)} %copy-done, ...), custom_call_target="tpu_custom_call" | custom-call | flops 67108864 | bytes 163840 | tf_op jit(solution)/shard_map/pallas_call | solution.py:252
  213.2 3.2 shard_map.114
  216.4 1.3 collective-permute-start.14
  217.7 2.1 collective-permute-start.15
  219.8 1.0 collective-permute-start.12
  220.9 8.6 %shard_map.111.own_ref = bf16[1024,1024]{1,0:T(8,128)(2,1)S(1)} custom-call(s32[6]{0:T(128)S(1)} %stack.46.pick, bf16[4,1024,512]{2,1,0:T(8,128)(2,1)} %bitcast.33, bf16[4,1024,512]{2,1,0:T(8,128)(2,1)} %bitcast.34, bf16[4,1024,512]{2,1,0:T(8,128)(2,1)} %bitcast.35, bf16[4,1024,512]{2,1,0:T(8,128)(2,1)} %bitcast.36, bf16[512,2048]{1,0:T(8,128)(2,1)S(1)} %copy-done, ...), custom_call_target="tpu_custom_call" | custom-call | flops 67108864 | bytes 163840 | tf_op jit(solution)/shard_map/pallas_call | solution.py:252
  229.5 8.6 %shard_map.110.own_ref = bf16[1024,1024]{1,0:T(8,128)(2,1)S(1)} custom-call(s32[6]{0:T(128)S(1)} %stack.46.pick, bf16[4,1024,512]{2,1,0:T(8,128)(2,1)} %bitcast.37, bf16[4,1024,512]{2,1,0:T(8,128)(2,1)} %bitcast.38, bf16[4,1024,512]{2,1,0:T(8,128)(2,1)} %bitcast.39, bf16[4,1024,512]{2,1,0:T(8,128)(2,1)} %bitcast.40, bf16[512,2048]{1,0:T(8,128)(2,1)S(1)} %copy-done, ...), custom_call_target="tpu_custom_call" | custom-call | flops 67108864 | bytes 163840 | tf_op jit(solution)/shard_map/pallas_call | solution.py:252
  238.1 12.6 %shard_map.112 = (bf16[1024,2048]{1,0:T(8,128)(2,1)}, bf16[1024,1024]{1,0:T(8,128)(2,1)S(1)}, bf16[128,1024]{1,0:T(8,128)(2,1)S(1)}, f32[64,256]{1,0:T(8,128)S(1)}) custom-call(bf16[1024,1024]{1,0:T(8,128)(2,1)S(1)} %shard_map.110.own_ref, bf16[1024,1024]{1,0:T(8,128)(2,1)} %collective-permute-done.10.refs_0_, bf16[1024,2048]{1,0:T(8,128)(2,1)} %refs_1_.3, ...), custom_call_target="tpu_custom_call" | custom-call | flops 67108864 | bytes 294912 | tf_op jit(solution)/shard_map/pallas_call | solution.py:172
  250.7 10.4 %collective-permute-done.14.outer_ref = bf16[512,2048]{1,0:T(8,128)(2,1)} collective-permute-done((bf16[512,2048]{1,0:T(8,128)(2,1)S(1)}, bf16[512,2048]{1,0:T(8,128)(2,1)}, u32[]{:S(2)}, u32[]{:S(2)}) %collective-permute-start.14) | collective-permute-done | bytes 2097184 | tf_op jit(solution)/shard_map/ppermute | solution.py:410
  261.1 0.5 collective-permute-done.15.inner_ref
  261.7 7.3 %shard_map.115 = (bf16[512,2048]{1,0:T(8,128)(2,1)}, bf16[512,2048]{1,0:T(8,128)(2,1)}) custom-call(s32[2]{0:T(128)S(1)} %add_convert_fusion.at, bf16[3,512,2048]{2,1,0:T(8,128)(2,1)} %shard_map.108.rows_ref, bf16[512,2048]{1,0:T(8,128)(2,1)} %collective-permute-done.14.outer_ref, bf16[512,2048]{1,0:T(8,128)(2,1)} %collective-permute-done.15.inner_ref, ...), custom_call_target="tpu_custom_call" | custom-call | flops 65536 | bytes 196608 | tf_op jit(solution)/shard_map/pallas_call | solution.py:365
  269.0 3.5 collective-permute-start.16
  272.5 3.7 %collective-permute-start.17 = (bf16[512,2048]{1,0:T(8,128)(2,1)}, bf16[512,2048]{1,0:T(8,128)(2,1)}, u32[]{:S(2)}, u32[]{:S(2)}) collective-permute-start(bf16[512,2048]{1,0:T(8,128)(2,1)} %get-tuple-element.127), channel_id=1, source_target_pairs={{8,0},{12,4},{16,8},{20,12},{24,16},{28,20},{9,1},{13,5},{17,9},{2... | collective-permute-start | bytes 6291464 | tf_op jit(solution)/shard_map/ppermute | solution.py:410
  276.2 1.9 collective-permute-start.18
  278.1 1.3 copy-done.13
  279.5 13.2 %shard_map.113 = (bf16[1024,2048]{1,0:T(8,128)(2,1)}, bf16[1024,1024]{1,0:T(8,128)(2,1)S(1)}, bf16[128,1024]{1,0:T(8,128)(2,1)}, f32[64,256]{1,0:T(8,128)S(1)}) custom-call(bf16[1024,1024]{1,0:T(8,128)(2,1)S(1)} %shard_map.111.own_ref, bf16[1024,1024]{1,0:T(8,128)(2,1)} %copy-done.13, bf16[1024,2048]{1,0:T(8,128)(2,1)} %refs_1_.3, ...), custom_call_target="tpu_custom_call", output_to_operand_aliasing={{0}: (7, {})} | custom-call | flops 67108864 | bytes 294912 | tf_op jit(solution)/shard_map/pallas_call | solution.py:172
  292.6 1.3 copy-done.9
  294.0 4.7 %collective-permute-start.13 = (bf16[128,1024]{1,0:T(8,128)(2,1)}, bf16[128,1024]{1,0:T(8,128)(2,1)S(1)}, u32[]{:S(2)}, u32[]{:S(2)}) collective-permute-start(bf16[128,1024]{1,0:T(8,128)(2,1)} %get-tuple-element.116), channel_id=1, source_target_pairs={{4,0},{8,4},{12,8},{16,12},{20,16},{24,20},{28,24},{5,1},{9,5},{13... | collective-permute-start | bytes 786440 | tf_op jit(solution)/shard_map/ppermute | solution.py:410
  298.8 0.7 copy.14
  299.6 6.2 %all-to-all-start = ((f32[8,16,128]{2,1,0:T(8,128)}), f32[8,16,128]{2,1,0:T(8,128)S(1)}, u32[]{:S(2)}, u32[]{:S(2)}) async-start(f32[8,16,128]{2,1,0:T(8,128)} %bitcast.16), calls=%async_computation | async-start | bytes 131072 | tf_op jit(solution)/shard_map/all_to_all | solution.py:557
  305.8 23.7 %all-to-all-done = f32[8,16,128]{2,1,0:T(8,128)S(1)} async-done(((f32[8,16,128]{2,1,0:T(8,128)}), f32[8,16,128]{2,1,0:T(8,128)S(1)}, u32[]{:S(2)}, u32[]{:S(2)}) %all-to-all-start) | async-done | bytes 65568 | tf_op jit(solution)/shard_map/all_to_all | solution.py:557
  329.5 0.6 reduce_sum.9
  330.1 10.4 %shard_map.116 = (bf16[1024,2048]{1,0:T(8,128)(2,1)}, bf16[1024,2048]{1,0:T(8,128)(2,1)}) custom-call(bf16[1024,1024]{1,0:T(8,128)(2,1)S(1)} %get-tuple-element.128.gm, bf16[128,1024]{1,0:T(8,128)(2,1)S(1)} %collective-permute-done.18.later, bf16[1024,2048]{1,0:T(8,128)(2,1)} %k.7, bf16[1024,2048]{1,0:T(8,128)(2,1)} %v.7, ...), custom_call_target="tpu_custom_call" | custom-call | flops 67108864 | bytes 229376 | tf_op jit(solution)/shard_map/pallas_call | solution.py:218
  340.6 5.0 %shard_map.118 = bf16[512,2048]{1,0:T(8,128)(2,1)} custom-call(bf16[3,512,2048]{2,1,0:T(8,128)(2,1)} %shard_map.108.rows_ref, bf16[512,2048]{1,0:T(8,128)(2,1)} %collective-permute-done.16.below, bf16[512,2048]{1,0:T(8,128)(2,1)} %collective-permute-done.17.above), custom_call_target="tpu_custom_call" | custom-call | flops 32768 | bytes 131072 | tf_op jit(solution)/shard_map/pallas_call | solution.py:389
  345.6 10.5 %shard_map.117 = (bf16[1024,2048]{1,0:T(8,128)(2,1)}, bf16[1024,2048]{1,0:T(8,128)(2,1)}) custom-call(bf16[1024,1024]{1,0:T(8,128)(2,1)S(1)} %copy-done.10, bf16[128,1024]{1,0:T(8,128)(2,1)S(1)} %collective-permute-done.13.later, bf16[1024,2048]{1,0:T(8,128)(2,1)} %k.7, bf16[1024,2048]{1,0:T(8,128)(2,1)} %v.7, ...), custom_call_target="tpu_custom_call", output_to_operand_aliasing={{0}: (5, {}), {1}: (6, {})} | custom-call | flops 67108864 | bytes 229376 | tf_op jit(solution)/shard_map/pallas_call | solution.py:218
  (47 shorter events, 0.7 us)
Async XLA Ops:
  7.2 72.8 %all-gather.5.cloned.1.call-start = ((), (), s32[]{:S(2)}) async-start(), calls=%async_computation.1 | async-start | bytes 5242880 | tf_op jit(solution)/shard_map/all_gather | solution.py:484
  8.6 19.7 %copy-start = (bf16[512,2048]{1,0:T(8,128)(2,1)S(1)}, bf16[512,2048]{1,0:T(8,128)(2,1)}, u32[]{:S(2)}) copy-start(bf16[512,2048]{1,0:T(8,128)(2,1)} %refs_4_.3) | copy-start | bytes 6291460
  8.6 27.6 %copy-start.14 = (bf16[128,128]{1,0:T(8,128)(2,1)S(1)}, bf16[128,128]{1,0:T(8,128)(2,1)}, u32[]{:S(2)}) copy-start(bf16[128,128]{1,0:T(8,128)(2,1)} %param.9) | copy-start | bytes 98308
  11.8 117.2 %all-gather.7.cloned.1.call-start = ((), (), s32[]{:S(2)}) async-start(), calls=%async_computation.2 | async-start | bytes 5242880 | tf_op jit(solution)/shard_map/all_gather | solution.py:497
  11.8 16.5 %collective-permute-start = (bf16[128,2048]{1,0:T(8,128)(2,1)S(1)}, bf16[128,2048]{1,0:T(8,128)(2,1)S(1)}, u32[]{:S(2)}, u32[]{:S(2)}) collective-permute-start(bf16[128,2048]{1,0:T(8,128)(2,1)S(1)} %multiply_convert_fusion), channel_id=1, source_target_pairs={{0,4},{4,8},{8,12},{12,16},{16,20},{20,24},{24,28},{1,5},{5,9},{9,... | collective-permute-start | bytes 1572872 | tf_op jit(solution)/shard_map/ppermute | solution.py:410
  28.3 48.5 %collective-permute-start.1 = (bf16[512,2048]{1,0:T(8,128)(2,1)S(1)}, bf16[512,2048]{1,0:T(8,128)(2,1)}, u32[]{:S(2)}, u32[]{:S(2)}) collective-permute-start(bf16[512,2048]{1,0:T(8,128)(2,1)S(1)} %copy-done), channel_id=1, source_target_pairs={{0,8},{4,12},{8,16},{12,20},{16,24},{20,28},{1,9},{5,13},{9,17},{1... | collective-permute-start | bytes 6291464 | tf_op jit(solution)/shard_map/ppermute | solution.py:410
  31.8 48.2 %collective-permute-start.2 = (bf16[512,2048]{1,0:T(8,128)(2,1)S(1)}, bf16[512,2048]{1,0:T(8,128)(2,1)}, u32[]{:S(2)}, u32[]{:S(2)}) collective-permute-start(bf16[512,2048]{1,0:T(8,128)(2,1)S(1)} %copy-done), channel_id=1, source_target_pairs={{8,0},{12,4},{16,8},{20,12},{24,16},{28,20},{9,1},{13,5},{17,9},{2... | collective-permute-start | bytes 6291464 | tf_op jit(solution)/shard_map/ppermute | solution.py:410
  35.5 37.0 %collective-permute-start.3 = (bf16[1024,512]{1,0:T(8,128)(2,1)}, bf16[1024,512]{1,0:T(8,128)(2,1)}, u32[]{:S(2)}, u32[]{:S(2)}) collective-permute-start(bf16[1024,512]{1,0:T(8,128)(2,1)} %get-tuple-element.74), channel_id=1, source_target_pairs={{0,4},{4,0},{8,12},{12,8},{16,20},{20,16},{24,28},{28,24},{1,5},{5... | collective-permute-start | bytes 3145736 | tf_op jit(solution)/shard_map/ppermute | solution.py:410
  57.3 1.3 copy-start.4
  58.7 1.3 copy-start.7
  69.9 1.3 copy-start.3
  71.2 1.3 copy-start.5
  80.0 48.9 %collective-permute-start.4 = (bf16[1024,1024]{1,0:T(8,128)(2,1)}, bf16[1024,1024]{1,0:T(8,128)(2,1)}, u32[]{:S(2)}, u32[]{:S(2)}) collective-permute-start(bf16[1024,1024]{1,0:T(8,128)(2,1)} %copy-done.7), channel_id=1, source_target_pairs={{0,4},{4,0},{8,12},{12,8},{16,20},{20,16},{24,28},{28,24},{1,5},{5... | collective-permute-start | bytes 6291464 | tf_op jit(solution)/shard_map/ppermute | solution.py:410
  80.8 52.0 %collective-permute-start.6 = (bf16[512,2048]{1,0:T(8,128)(2,1)}, bf16[512,2048]{1,0:T(8,128)(2,1)}, u32[]{:S(2)}, u32[]{:S(2)}) collective-permute-start(bf16[512,2048]{1,0:T(8,128)(2,1)} %collective-permute-done.1.refs_5_), channel_id=1, source_target_pairs={{8,16},{12,20},{16,24},{20,28},{9,17},{13,21},{17,25},{21,29},{10,... | collective-permute-start | bytes 6291464 | tf_op jit(solution)/shard_map/ppermute | solution.py:410
  85.7 47.1 %collective-permute-start.7 = (bf16[512,2048]{1,0:T(8,128)(2,1)}, bf16[512,2048]{1,0:T(8,128)(2,1)}, u32[]{:S(2)}, u32[]{:S(2)}) collective-permute-start(bf16[512,2048]{1,0:T(8,128)(2,1)} %collective-permute-done.2.refs_6_), channel_id=1, source_target_pairs={{16,8},{20,12},{8,0},{12,4},{17,9},{21,13},{9,1},{13,5},{18,10},{2... | collective-permute-start | bytes 6291464 | tf_op jit(solution)/shard_map/ppermute | solution.py:410
  87.6 83.0 %collective-permute-start.5 = (bf16[1024,1024]{1,0:T(8,128)(2,1)}, bf16[1024,1024]{1,0:T(8,128)(2,1)}, u32[]{:S(2)}, u32[]{:S(2)}) collective-permute-start(bf16[1024,1024]{1,0:T(8,128)(2,1)} %copy-done.5), channel_id=1, source_target_pairs={{0,4},{4,0},{8,12},{12,8},{16,20},{20,16},{24,28},{28,24},{1,5},{5... | collective-permute-start | bytes 6291464 | tf_op jit(solution)/shard_map/ppermute | solution.py:410
  89.0 1.7 copy-start.6
  90.7 1.6 copy-start.8
  132.8 8.6 %copy-start.1 = (bf16[1,512,1024]{2,1,0:T(8,128)(2,1)}, bf16[1,512,1024]{2,1,0:T(8,128)(2,1)S(1)}, u32[]{:S(2)}) copy-start(bf16[1,512,1024]{2,1,0:T(8,128)(2,1)S(1)} %shard_map.105) | copy-start | bytes 3145732
  136.3 43.7 %collective-permute-start.9 = (bf16[512,2048]{1,0:T(8,128)(2,1)}, bf16[512,2048]{1,0:T(8,128)(2,1)}, u32[]{:S(2)}, u32[]{:S(2)}) collective-permute-start(bf16[512,2048]{1,0:T(8,128)(2,1)} %broadcast_select_fusion.refs_7_), channel_id=1, source_target_pairs={{16,24},{20,28},{8,0},{12,4},{17,25},{21,29},{9,1},{13,5},{18,26},... | collective-permute-start | bytes 6291464 | tf_op jit(solution)/shard_map/ppermute | solution.py:410
  141.4 29.2 %collective-permute-start.8 = (bf16[512,1024]{1,0:T(8,128)(2,1)S(1)}, bf16[512,1024]{1,0:T(8,128)(2,1)S(1)}, u32[]{:S(2)}, u32[]{:S(2)}) collective-permute-start(bf16[512,1024]{1,0:T(8,128)(2,1)S(1)} %bitcast.19), channel_id=1, source_target_pairs={{0,8},{4,12},{24,16},{28,20},{1,9},{5,13},{25,17},{29,21},{2,10},{... | collective-permute-start | bytes 3145736 | tf_op jit(solution)/shard_map/ppermute | solution.py:410
  170.6 1.0 copy-start.11
  176.4 36.8 %collective-permute-start.11 = (bf16[512,1024]{1,0:T(8,128)(2,1)}, bf16[512,1024]{1,0:T(8,128)(2,1)}, u32[]{:S(2)}, u32[]{:S(2)}) collective-permute-start(bf16[512,1024]{1,0:T(8,128)(2,1)} %bitcast.12.refs_1_), channel_id=1, source_target_pairs={{0,8},{4,12},{24,16},{28,20},{1,9},{5,13},{25,17},{29,21},{2,10},{... | collective-permute-start | bytes 3145736 | tf_op jit(solution)/shard_map/ppermute | solution.py:410
  188.6 49.5 %collective-permute-start.10 = (bf16[1024,1024]{1,0:T(8,128)(2,1)S(1)}, bf16[1024,1024]{1,0:T(8,128)(2,1)}, u32[]{:S(2)}, u32[]{:S(2)}) collective-permute-start(bf16[1024,1024]{1,0:T(8,128)(2,1)S(1)} %shard_map.107), channel_id=1, source_target_pairs={{0,4},{4,0},{8,12},{12,8},{16,20},{20,16},{24,28},{28,24},{1,5},{5... | collective-permute-start | bytes 6291464 | tf_op jit(solution)/shard_map/ppermute | solution.py:410
  204.6 8.6 %copy-start.12 = (bf16[512,1024]{1,0:T(8,128)(2,1)S(1)}, bf16[512,1024]{1,0:T(8,128)(2,1)}, u32[]{:S(2)}) copy-start(bf16[512,1024]{1,0:T(8,128)(2,1)} %copy-done.11) | copy-start | bytes 3145732
  216.4 44.7 %collective-permute-start.14 = (bf16[512,2048]{1,0:T(8,128)(2,1)S(1)}, bf16[512,2048]{1,0:T(8,128)(2,1)}, u32[]{:S(2)}, u32[]{:S(2)}) collective-permute-start(bf16[512,2048]{1,0:T(8,128)(2,1)S(1)} %shard_map.114), channel_id=1, source_target_pairs={{0,8},{4,12},{24,16},{28,20},{1,9},{5,13},{25,17},{29,21},{2,10},{... | collective-permute-start | bytes 6291464 | tf_op jit(solution)/shard_map/ppermute | solution.py:410
  217.7 44.0 %collective-permute-start.15 = (bf16[512,2048]{1,0:T(8,128)(2,1)S(1)}, bf16[512,2048]{1,0:T(8,128)(2,1)}, u32[]{:S(2)}, u32[]{:S(2)}) collective-permute-start(bf16[512,2048]{1,0:T(8,128)(2,1)S(1)} %shard_map.114), channel_id=1, source_target_pairs={{8,16},{12,20},{16,8},{20,12},{9,17},{13,21},{17,9},{21,13},{10,18... | collective-permute-start | bytes 6291464 | tf_op jit(solution)/shard_map/ppermute | solution.py:410
  219.8 58.3 %collective-permute-start.12 = (bf16[1024,1024]{1,0:T(8,128)(2,1)S(1)}, bf16[1024,1024]{1,0:T(8,128)(2,1)S(1)}, u32[]{:S(2)}, u32[]{:S(2)}) collective-permute-start(bf16[1024,1024]{1,0:T(8,128)(2,1)S(1)} %shard_map.109), channel_id=1, source_target_pairs={{0,4},{4,0},{8,12},{12,8},{16,20},{20,16},{24,28},{28,24},{1,5},{5... | collective-permute-start | bytes 6291464 | tf_op jit(solution)/shard_map/ppermute | solution.py:410
  238.1 23.6 %copy-start.2 = (bf16[1,512,1024]{2,1,0:T(8,128)(2,1)S(1)}, bf16[1,512,1024]{2,1,0:T(8,128)(2,1)}, u32[]{:S(2)}) copy-start(bf16[1,512,1024]{2,1,0:T(8,128)(2,1)} %copy-done.1) | copy-start | bytes 3145732
  269.0 71.6 %collective-permute-start.16 = (bf16[512,2048]{1,0:T(8,128)(2,1)}, bf16[512,2048]{1,0:T(8,128)(2,1)}, u32[]{:S(2)}, u32[]{:S(2)}) collective-permute-start(bf16[512,2048]{1,0:T(8,128)(2,1)} %get-tuple-element.126), channel_id=1, source_target_pairs={{0,8},{4,12},{8,16},{12,20},{16,24},{20,28},{1,9},{5,13},{9,17},{1... | collective-permute-start | bytes 6291464 | tf_op jit(solution)/shard_map/ppermute | solution.py:410
  272.5 68.1 %collective-permute-start.17 = (bf16[512,2048]{1,0:T(8,128)(2,1)}, bf16[512,2048]{1,0:T(8,128)(2,1)}, u32[]{:S(2)}, u32[]{:S(2)}) collective-permute-start(bf16[512,2048]{1,0:T(8,128)(2,1)} %get-tuple-element.127), channel_id=1, source_target_pairs={{8,0},{12,4},{16,8},{20,12},{24,16},{28,20},{9,1},{13,5},{17,9},{2... | collective-permute-start | bytes 6291464 | tf_op jit(solution)/shard_map/ppermute | solution.py:410
  276.2 53.9 %collective-permute-start.18 = (bf16[128,1024]{1,0:T(8,128)(2,1)S(1)}, bf16[128,1024]{1,0:T(8,128)(2,1)S(1)}, u32[]{:S(2)}, u32[]{:S(2)}) collective-permute-start(bf16[128,1024]{1,0:T(8,128)(2,1)S(1)} %get-tuple-element.108), channel_id=1, source_target_pairs={{4,0},{8,4},{12,8},{16,12},{20,16},{24,20},{28,24},{5,1},{9,5},{13... | collective-permute-start | bytes 786440 | tf_op jit(solution)/shard_map/ppermute | solution.py:410
  278.1 1.3 copy-start.13
  292.6 1.3 copy-start.9
  294.0 51.6 %collective-permute-start.13 = (bf16[128,1024]{1,0:T(8,128)(2,1)}, bf16[128,1024]{1,0:T(8,128)(2,1)S(1)}, u32[]{:S(2)}, u32[]{:S(2)}) collective-permute-start(bf16[128,1024]{1,0:T(8,128)(2,1)} %get-tuple-element.116), channel_id=1, source_target_pairs={{4,0},{8,4},{12,8},{16,12},{20,16},{24,20},{28,24},{5,1},{9,5},{13... | collective-permute-start | bytes 786440 | tf_op jit(solution)/shard_map/ppermute | solution.py:410
  299.6 29.9 %all-to-all-start = ((f32[8,16,128]{2,1,0:T(8,128)}), f32[8,16,128]{2,1,0:T(8,128)S(1)}, u32[]{:S(2)}, u32[]{:S(2)}) async-start(f32[8,16,128]{2,1,0:T(8,128)} %bitcast.16), calls=%async_computation | async-start | bytes 131072 | tf_op jit(solution)/shard_map/all_to_all | solution.py:557
  340.6 5.0 %copy-start.10 = (bf16[1024,1024]{1,0:T(8,128)(2,1)S(1)}, bf16[1024,1024]{1,0:T(8,128)(2,1)}, u32[]{:S(2)}) copy-start(bf16[1024,1024]{1,0:T(8,128)(2,1)} %copy-done.9) | copy-start | bytes 6291460
Sparse Core Ops, SparseCore 0:
  11.9 34.6 all-gather.4
  80.1 32.8 all-gather.6
